TPU v7x, 128 devices: a whole 4x4x4 slice. The times are simulated.
128 devices in a mesh: inst: 16 (over z_hi, y, core), tp: 8 (over x, z_lo).
Axes of the slice: x: 4, y: 4, z: 4 (z_hi: 2, z_lo: 2; z = z_hi * 2 + z_lo), core: 2. Of those that a mesh axis runs over, the one named last changes fastest.
Arguments:
- q_prefill: bfloat16 [16384, 4096], P('inst', 'tp'), may hold values from -70 to 70
- k_prefill: bfloat16 [16384, 1024], P('inst', 'tp'), may hold values from -6 to 6
- v_prefill: bfloat16 [16384, 1024], P('inst', 'tp'), may hold values from -6 to 6
- q_decode: bfloat16 [2, 128, 4096], P(None, 'inst', 'tp'), may hold values from -70 to 70
- k_new: bfloat16 [2, 128, 1024], P(None, 'inst', 'tp'), may hold values from -6 to 6
- v_new: bfloat16 [2, 128, 1024], P(None, 'inst', 'tp'), may hold values from -6 to 6
- k_cache: bfloat16 [2048, 128, 1024], P('inst', None, 'tp'), may hold values from -6 to 6
- v_cache: bfloat16 [2048, 128, 1024], P('inst', None, 'tp'), may hold values from -6 to 6
- block_table: int32 [128, 16], replicated, may hold values from 0 to 2047, as said below
- req_lengths: int32 [128], replicated, may hold values from 1 to 2048, 157286 in all
Outputs:
- prefill_out: bfloat16 [16384, 4096], P('inst', 'tp')
- decode_out: bfloat16 [2, 128, 4096], P(None, 'inst', 'tp')
Inputs may be any that keep to these rules, and one draw needn't show every extreme that they name: `block_table`: each block number appears exactly once in the table.
All inputs are finite; a program needn't handle non-finite values.
Results may differ from a plain program's by a relative error of at most 0.009.
Values may be sent and summed in bfloat16 or wider, within the bound.
No kernel may reach another device: no remote copies, remote signals or barrier semaphores. Data moves between devices by JAX's collectives and lax.ppermute only.
A program may use at most 128 MiB of HBM per device.

v0:
```python
import jax
import jax.numpy as jnp
from jax import lax
from jax.sharding import PartitionSpec as P

HD = 128


def shifted(value, axis, steps):
    count = lax.axis_size(axis)
    leading, last = (max(0, -steps), min(count, count - steps))
    return lax.ppermute(value, axis, [(source, source + steps) for source in range(leading, last)])


def combined_all(value, axis, join):
    pieces = jax.tree.map(lambda part: lax.all_gather(part, axis), value)
    head = jax.tree.map(lambda part: part[0], pieces)
    tail = jax.tree.map(lambda part: part[1:], pieces)
    so_far, _ = lax.scan(lambda so_far, share: (join(so_far, share), None), head, tail)
    return so_far


def combine_parts(first_part, second_part):
    top_a, sum_a, out_a = first_part
    top_b, sum_b, out_b = second_part
    top_new = jnp.maximum(top_a, top_b)
    factor_a = jnp.exp(top_a - top_new)
    factor_b = jnp.exp(top_b - top_new)
    return (
        top_new,
        sum_a * factor_a + sum_b * factor_b,
        out_a * factor_a[..., None] + out_b * factor_b[..., None],
    )


def prefill_part(q_prefill, k_prefill, v_prefill):
    row_count = q_prefill.shape[0]
    head_kv = k_prefill.shape[1] // HD
    group_size = q_prefill.shape[1] // k_prefill.shape[1]
    softmax_scale = HD ** (-0.5)
    queries = q_prefill.reshape(row_count, head_kv, group_size, HD)
    my_index = lax.axis_index("inst")
    query_pos = my_index * row_count + jnp.arange(row_count, dtype=jnp.int32)
    initial = (
        jnp.full((row_count, head_kv, group_size), -1e30, jnp.float32),
        jnp.zeros((row_count, head_kv, group_size), jnp.float32),
        jnp.zeros((row_count, head_kv, group_size, HD), jnp.float32),
    )

    def attend(running, key_rows, value_rows, key_pos):
        key_rows = key_rows.reshape(key_rows.shape[0], head_kv, HD)
        value_rows = value_rows.reshape(value_rows.shape[0], head_kv, HD)
        scores = (
            jnp.einsum("tkgd,skd->tkgs", queries, key_rows, preferred_element_type=jnp.float32)
            * softmax_scale
        )
        allowed = (key_pos[None, :] <= query_pos[:, None])[:, None, None, :]
        scores = jnp.where(allowed, scores, -1e30)
        run_top, run_sum, run_out = running
        top_new = jnp.maximum(run_top, jnp.max(scores, axis=-1))
        factor = jnp.exp(run_top - top_new)
        weights = jnp.where(allowed, jnp.exp(scores - top_new[..., None]), 0.0)
        run_sum = run_sum * factor + jnp.sum(weights, axis=-1)
        mixed = jnp.einsum(
            "tkgs,skd->tkgd",
            weights.astype(jnp.bfloat16),
            value_rows,
            preferred_element_type=jnp.float32,
        )
        run_out = run_out * factor[..., None] + mixed
        return (top_new, run_sum, run_out)

    both_kv = jnp.stack([k_prefill, v_prefill])
    running = attend(initial, k_prefill, v_prefill, query_pos)

    def relay_turn(step, state):
        held_kv, running = state
        held_kv = shifted(held_kv, "inst", 1)
        key_pos = (my_index - step) * row_count + jnp.arange(row_count, dtype=jnp.int32)
        running = lax.cond(
            my_index >= step,
            lambda state_in: attend(state_in, held_kv[0], held_kv[1], key_pos),
            lambda state_in: state_in,
            running,
        )
        return (held_kv, running)

    held_kv, running = lax.fori_loop(1, lax.axis_size("inst"), relay_turn, (both_kv, running))
    run_top, run_sum, run_out = running
    result = run_out / run_sum[..., None]
    return result.reshape(row_count, q_prefill.shape[1]).astype(jnp.bfloat16)


def decode_part(q_decode, k_new, v_new, k_cache, v_cache, block_table, req_lengths):
    step_count, req_local, query_width = q_decode.shape
    head_kv = k_cache.shape[2] // HD
    group_size = query_width // k_cache.shape[2]
    blocks_local, block_len = (k_cache.shape[0], k_cache.shape[1])
    softmax_scale = HD ** (-0.5)
    my_index = lax.axis_index("inst")
    every_query = lax.all_gather(q_decode, "inst", axis=1, tiled=True)
    total_req = every_query.shape[1]
    table_width = block_table.shape[1]
    global_id = my_index * blocks_local + jnp.arange(blocks_local, dtype=jnp.int32)
    matches = block_table.reshape(-1)[None, :] == global_id[:, None]
    flat_index = jnp.sum(
        jnp.where(matches, jnp.arange(total_req * table_width, dtype=jnp.int32)[None, :], 0), axis=1
    )
    owner_req = flat_index // table_width
    logical = flat_index % table_width
    positions = logical[:, None] * block_len + jnp.arange(block_len, dtype=jnp.int32)[None, :]
    valid_slot = positions < req_lengths[owner_req][:, None]
    belongs = owner_req[None, :] == jnp.arange(total_req, dtype=jnp.int32)[:, None]
    key_rows = k_cache.reshape(blocks_local, block_len, head_kv, HD)
    value_rows = v_cache.reshape(blocks_local, block_len, head_kv, HD)
    results = []
    for step in range(step_count):
        query_step = every_query[step].reshape(total_req, head_kv, group_size, HD)
        query_blk = query_step[owner_req]
        scores = (
            jnp.einsum("bkgd,bskd->bkgs", query_blk, key_rows, preferred_element_type=jnp.float32)
            * softmax_scale
        )
        live = valid_slot[:, None, None, :]
        scores = jnp.where(live, scores, -1e30)
        block_top = jnp.max(scores, axis=-1)
        req_top = jnp.max(jnp.where(belongs[:, :, None, None], block_top[None], -1e30), axis=1)
        weights = jnp.where(live, jnp.exp(scores - req_top[owner_req][..., None]), 0.0)
        block_sum = jnp.sum(weights, axis=-1)
        block_out = jnp.einsum(
            "bkgs,bskd->bkgd",
            weights.astype(jnp.bfloat16),
            value_rows,
            preferred_element_type=jnp.float32,
        )
        req_sum = jax.ops.segment_sum(block_sum, owner_req, num_segments=total_req)
        req_out = jax.ops.segment_sum(block_out, owner_req, num_segments=total_req)
        merged = combined_all((req_top, req_sum, req_out), "inst", combine_parts)
        own_top, own_sum, own_out = [
            lax.dynamic_slice_in_dim(piece, my_index * req_local, req_local, 0) for piece in merged
        ]
        running = (own_top, own_sum, own_out)
        own_query = q_decode[step].reshape(req_local, head_kv, group_size, HD)
        for token in range(step + 1):
            new_key = k_new[token].reshape(req_local, head_kv, HD)
            new_value = v_new[token].reshape(req_local, head_kv, HD).astype(jnp.float32)
            new_score = (
                jnp.einsum("rkgd,rkd->rkg", own_query, new_key, preferred_element_type=jnp.float32)
                * softmax_scale
            )
            new_part = (
                new_score,
                jnp.ones_like(new_score),
                jnp.broadcast_to(new_value[:, :, None, :], (req_local, head_kv, group_size, HD)),
            )
            running = combine_parts(running, new_part)
        final_top, final_sum, final_out = running
        results.append((final_out / final_sum[..., None]).reshape(req_local, query_width))
    return jnp.stack(results).astype(jnp.bfloat16)


def body(
    q_prefill,
    k_prefill,
    v_prefill,
    q_decode,
    k_new,
    v_new,
    k_cache,
    v_cache,
    block_table,
    req_lengths,
):
    prefill_out = prefill_part(q_prefill, k_prefill, v_prefill)
    decode_out = decode_part(q_decode, k_new, v_new, k_cache, v_cache, block_table, req_lengths)
    return (prefill_out, decode_out)


def solution(mesh):
    placed = (
        P("inst", "tp"),
        P("inst", "tp"),
        P("inst", "tp"),
        P(None, "inst", "tp"),
        P(None, "inst", "tp"),
        P(None, "inst", "tp"),
        P("inst", None, "tp"),
        P("inst", None, "tp"),
        P(),
        P(),
    )
    return jax.shard_map(
        body,
        mesh=mesh,
        in_specs=placed,
        out_specs=(P("inst", "tp"), P(None, "inst", "tp")),
        check_vma=False,
    )
```

profile of v0, /device:TPU:121, one launch (start us, length us, event | category | flops | bytes accessed | tf_op | source)
XLA Modules:
  0.0 674.8 jit_solution(7153743962582023404)
XLA Ops:
  8.5 19.5 %all_gather.39 = bf16[2,128,512]{2,1,0:T(8,128)(2,1)S(1)} all-gather(bf16[2,8,512]{2,1,0:T(8,128)(2,1)} %param.21), channel_id=1, replica_groups=mesh['inst'=16,'tp'=8] {'inst'}, dimensions={1}, use_global_device_ids=true | all-gather | bytes 278528 | tf_op jit(solution)/shard_map/all_gather | solution.py:101
  62.1 25.5 %all-gather.4 = f32[2048,4]{1,0:T(8,128)S(1)} all-gather(f32[128,4]{1,0:T(8,128)S(1)} %scatter_custom_fusion.2), channel_id=6, replica_groups=mesh['inst'=16,'tp'=8] {'inst'}, dimensions={0}, use_global_device_ids=true | all-gather | bytes 34816 | tf_op jit(solution)/shard_map/all_gather | solution.py:16
  87.7 20.3 %all-gather.3 = f32[2048,4]{0,1:T(4,128)S(1)} all-gather(f32[128,4]{0,1:T(4,128)S(1)} %get-tuple-element.445), channel_id=5, replica_groups=mesh['inst'=16,'tp'=8] {'inst'}, dimensions={0}, use_global_device_ids=true | all-gather | bytes 34816 | tf_op jit(solution)/shard_map/all_gather | solution.py:16
  110.2 24.3 %all-gather.1 = f32[2048,4]{1,0:T(8,128)S(1)} all-gather(f32[128,4]{1,0:T(8,128)S(1)} %scatter_custom_fusion), channel_id=3, replica_groups=mesh['inst'=16,'tp'=8] {'inst'}, dimensions={0}, use_global_device_ids=true | all-gather | bytes 34816 | tf_op jit(solution)/shard_map/all_gather | solution.py:16
  134.5 20.3 %all-gather = f32[2048,4]{0,1:T(4,128)S(1)} all-gather(f32[128,4]{0,1:T(4,128)S(1)} %get-tuple-element.444), channel_id=2, replica_groups=mesh['inst'=16,'tp'=8] {'inst'}, dimensions={0}, use_global_device_ids=true | all-gather | bytes 34816 | tf_op jit(solution)/shard_map/all_gather | solution.py:16
  184.9 367.5 %while.50 = (s32[]{:T(128)}, bf16[2,1024,128]{2,1,0:T(8,128)(2,1)S(1)}, f32[1024,1,4]{0,2,1:T(4,128)S(1)}, f32[1024,1,4]{0,2,1:T(4,128)S(1)}, f32[1024,1,4,128]{...) while((s32[]{:T(128)}, ...), condition=%wide.region_7.8_spmd.clone, body=%wide.region_2.7_spmd.clone.sunk | while | flops 2204121088 | bytes 80507248 | solution.py:88
  188.9 13.8 %conditional.3 = ((f32[1024,1,4]{0,2,1:T(4,128)S(1)}, f32[1024,1,4]{0,2,1:T(4,128)S(1)}, f32[1024,1,4,128]{3,0,2,1:T(8,128)})) conditional(s32[]{:T(128)} %convert_element_type.84, (f32[1024,1,4]{0,2,1:T(4,128)S(1)}, f32[1024,1,4]{0,2,1:T(4,128)S(1)}, f32[1024,1,4,128]{3,0,2,1:T(8,128)}) %tuple.128, (s32[]{:T(128)}, s32[]{:T(128)}, ...), branch_computations={%region_3.3_spmd, %region_4.6_spmd} | conditional | flops 2204121088 | bytes 77357176 | solution.py:80
  212.9 13.8 %conditional.3 = ((f32[1024,1,4]{0,2,1:T(4,128)S(1)}, f32[1024,1,4]{0,2,1:T(4,128)S(1)}, f32[1024,1,4,128]{3,0,2,1:T(8,128)})) conditional(s32[]{:T(128)} %convert_element_type.84, (f32[1024,1,4]{0,2,1:T(4,128)S(1)}, f32[1024,1,4]{0,2,1:T(4,128)S(1)}, f32[1024,1,4,128]{3,0,2,1:T(8,128)}) %tuple.128, (s32[]{:T(128)}, s32[]{:T(128)}, ...), branch_computations={%region_3.3_spmd, %region_4.6_spmd} | conditional | flops 2204121088 | bytes 77357176 | solution.py:80
  237.3 13.8 %conditional.3 = ((f32[1024,1,4]{0,2,1:T(4,128)S(1)}, f32[1024,1,4]{0,2,1:T(4,128)S(1)}, f32[1024,1,4,128]{3,0,2,1:T(8,128)})) conditional(s32[]{:T(128)} %convert_element_type.84, (f32[1024,1,4]{0,2,1:T(4,128)S(1)}, f32[1024,1,4]{0,2,1:T(4,128)S(1)}, f32[1024,1,4,128]{3,0,2,1:T(8,128)}) %tuple.128, (s32[]{:T(128)}, s32[]{:T(128)}, ...), branch_computations={%region_3.3_spmd, %region_4.6_spmd} | conditional | flops 2204121088 | bytes 77357176 | solution.py:80
  261.7 13.8 %conditional.3 = ((f32[1024,1,4]{0,2,1:T(4,128)S(1)}, f32[1024,1,4]{0,2,1:T(4,128)S(1)}, f32[1024,1,4,128]{3,0,2,1:T(8,128)})) conditional(s32[]{:T(128)} %convert_element_type.84, (f32[1024,1,4]{0,2,1:T(4,128)S(1)}, f32[1024,1,4]{0,2,1:T(4,128)S(1)}, f32[1024,1,4,128]{3,0,2,1:T(8,128)}) %tuple.128, (s32[]{:T(128)}, s32[]{:T(128)}, ...), branch_computations={%region_3.3_spmd, %region_4.6_spmd} | conditional | flops 2204121088 | bytes 77357176 | solution.py:80
  286.1 13.8 %conditional.3 = ((f32[1024,1,4]{0,2,1:T(4,128)S(1)}, f32[1024,1,4]{0,2,1:T(4,128)S(1)}, f32[1024,1,4,128]{3,0,2,1:T(8,128)})) conditional(s32[]{:T(128)} %convert_element_type.84, (f32[1024,1,4]{0,2,1:T(4,128)S(1)}, f32[1024,1,4]{0,2,1:T(4,128)S(1)}, f32[1024,1,4,128]{3,0,2,1:T(8,128)}) %tuple.128, (s32[]{:T(128)}, s32[]{:T(128)}, ...), branch_computations={%region_3.3_spmd, %region_4.6_spmd} | conditional | flops 2204121088 | bytes 77357176 | solution.py:80
  310.5 13.8 %conditional.3 = ((f32[1024,1,4]{0,2,1:T(4,128)S(1)}, f32[1024,1,4]{0,2,1:T(4,128)S(1)}, f32[1024,1,4,128]{3,0,2,1:T(8,128)})) conditional(s32[]{:T(128)} %convert_element_type.84, (f32[1024,1,4]{0,2,1:T(4,128)S(1)}, f32[1024,1,4]{0,2,1:T(4,128)S(1)}, f32[1024,1,4,128]{3,0,2,1:T(8,128)}) %tuple.128, (s32[]{:T(128)}, s32[]{:T(128)}, ...), branch_computations={%region_3.3_spmd, %region_4.6_spmd} | conditional | flops 2204121088 | bytes 77357176 | solution.py:80
  334.9 13.8 %conditional.3 = ((f32[1024,1,4]{0,2,1:T(4,128)S(1)}, f32[1024,1,4]{0,2,1:T(4,128)S(1)}, f32[1024,1,4,128]{3,0,2,1:T(8,128)})) conditional(s32[]{:T(128)} %convert_element_type.84, (f32[1024,1,4]{0,2,1:T(4,128)S(1)}, f32[1024,1,4]{0,2,1:T(4,128)S(1)}, f32[1024,1,4,128]{3,0,2,1:T(8,128)}) %tuple.128, (s32[]{:T(128)}, s32[]{:T(128)}, ...), branch_computations={%region_3.3_spmd, %region_4.6_spmd} | conditional | flops 2204121088 | bytes 77357176 | solution.py:80
  359.3 13.8 %conditional.3 = ((f32[1024,1,4]{0,2,1:T(4,128)S(1)}, f32[1024,1,4]{0,2,1:T(4,128)S(1)}, f32[1024,1,4,128]{3,0,2,1:T(8,128)})) conditional(s32[]{:T(128)} %convert_element_type.84, (f32[1024,1,4]{0,2,1:T(4,128)S(1)}, f32[1024,1,4]{0,2,1:T(4,128)S(1)}, f32[1024,1,4,128]{3,0,2,1:T(8,128)}) %tuple.128, (s32[]{:T(128)}, s32[]{:T(128)}, ...), branch_computations={%region_3.3_spmd, %region_4.6_spmd} | conditional | flops 2204121088 | bytes 77357176 | solution.py:80
  383.6 13.8 %conditional.3 = ((f32[1024,1,4]{0,2,1:T(4,128)S(1)}, f32[1024,1,4]{0,2,1:T(4,128)S(1)}, f32[1024,1,4,128]{3,0,2,1:T(8,128)})) conditional(s32[]{:T(128)} %convert_element_type.84, (f32[1024,1,4]{0,2,1:T(4,128)S(1)}, f32[1024,1,4]{0,2,1:T(4,128)S(1)}, f32[1024,1,4,128]{3,0,2,1:T(8,128)}) %tuple.128, (s32[]{:T(128)}, s32[]{:T(128)}, ...), branch_computations={%region_3.3_spmd, %region_4.6_spmd} | conditional | flops 2204121088 | bytes 77357176 | solution.py:80
  408.0 13.8 %conditional.3 = ((f32[1024,1,4]{0,2,1:T(4,128)S(1)}, f32[1024,1,4]{0,2,1:T(4,128)S(1)}, f32[1024,1,4,128]{3,0,2,1:T(8,128)})) conditional(s32[]{:T(128)} %convert_element_type.84, (f32[1024,1,4]{0,2,1:T(4,128)S(1)}, f32[1024,1,4]{0,2,1:T(4,128)S(1)}, f32[1024,1,4,128]{3,0,2,1:T(8,128)}) %tuple.128, (s32[]{:T(128)}, s32[]{:T(128)}, ...), branch_computations={%region_3.3_spmd, %region_4.6_spmd} | conditional | flops 2204121088 | bytes 77357176 | solution.py:80
  432.4 13.8 %conditional.3 = ((f32[1024,1,4]{0,2,1:T(4,128)S(1)}, f32[1024,1,4]{0,2,1:T(4,128)S(1)}, f32[1024,1,4,128]{3,0,2,1:T(8,128)})) conditional(s32[]{:T(128)} %convert_element_type.84, (f32[1024,1,4]{0,2,1:T(4,128)S(1)}, f32[1024,1,4]{0,2,1:T(4,128)S(1)}, f32[1024,1,4,128]{3,0,2,1:T(8,128)}) %tuple.128, (s32[]{:T(128)}, s32[]{:T(128)}, ...), branch_computations={%region_3.3_spmd, %region_4.6_spmd} | conditional | flops 2204121088 | bytes 77357176 | solution.py:80
  456.8 13.8 %conditional.3 = ((f32[1024,1,4]{0,2,1:T(4,128)S(1)}, f32[1024,1,4]{0,2,1:T(4,128)S(1)}, f32[1024,1,4,128]{3,0,2,1:T(8,128)})) conditional(s32[]{:T(128)} %convert_element_type.84, (f32[1024,1,4]{0,2,1:T(4,128)S(1)}, f32[1024,1,4]{0,2,1:T(4,128)S(1)}, f32[1024,1,4,128]{3,0,2,1:T(8,128)}) %tuple.128, (s32[]{:T(128)}, s32[]{:T(128)}, ...), branch_computations={%region_3.3_spmd, %region_4.6_spmd} | conditional | flops 2204121088 | bytes 77357176 | solution.py:80
  482.4 13.8 %conditional.3 = ((f32[1024,1,4]{0,2,1:T(4,128)S(1)}, f32[1024,1,4]{0,2,1:T(4,128)S(1)}, f32[1024,1,4,128]{3,0,2,1:T(8,128)})) conditional(s32[]{:T(128)} %convert_element_type.84, (f32[1024,1,4]{0,2,1:T(4,128)S(1)}, f32[1024,1,4]{0,2,1:T(4,128)S(1)}, f32[1024,1,4,128]{3,0,2,1:T(8,128)}) %tuple.128, (s32[]{:T(128)}, s32[]{:T(128)}, ...), branch_computations={%region_3.3_spmd, %region_4.6_spmd} | conditional | flops 2204121088 | bytes 77357176 | solution.py:80
  497.6 12.8 %collective-permute-done = bf16[2,1024,128]{2,1,0:T(8,128)(2,1)S(1)} collective-permute-done((bf16[2,1024,128]{2,1,0:T(8,128)(2,1)S(1)}, bf16[2,1024,128]{2,1,0:T(8,128)(2,1)S(1)}, u32[]{:S(2)}, u32[]{:S(2)}) %collective-permute-start) | collective-permute-done | bytes 524320 | tf_op jit(solution)/shard_map/while/body/eval_jaxpr/ppermute | solution.py:12
  510.4 13.8 %conditional.3 = ((f32[1024,1,4]{0,2,1:T(4,128)S(1)}, f32[1024,1,4]{0,2,1:T(4,128)S(1)}, f32[1024,1,4,128]{3,0,2,1:T(8,128)})) conditional(s32[]{:T(128)} %convert_element_type.84, (f32[1024,1,4]{0,2,1:T(4,128)S(1)}, f32[1024,1,4]{0,2,1:T(4,128)S(1)}, f32[1024,1,4,128]{3,0,2,1:T(8,128)}) %tuple.128, (s32[]{:T(128)}, s32[]{:T(128)}, ...), branch_computations={%region_3.3_spmd, %region_4.6_spmd} | conditional | flops 2204121088 | bytes 77357176 | solution.py:80
  538.4 13.8 %conditional.3 = ((f32[1024,1,4]{0,2,1:T(4,128)S(1)}, f32[1024,1,4]{0,2,1:T(4,128)S(1)}, f32[1024,1,4,128]{3,0,2,1:T(8,128)})) conditional(s32[]{:T(128)} %convert_element_type.84, (f32[1024,1,4]{0,2,1:T(4,128)S(1)}, f32[1024,1,4]{0,2,1:T(4,128)S(1)}, f32[1024,1,4,128]{3,0,2,1:T(8,128)}) %tuple.128, (s32[]{:T(128)}, s32[]{:T(128)}, ...), branch_computations={%region_3.3_spmd, %region_4.6_spmd} | conditional | flops 2204121088 | bytes 77357176 | solution.py:80
  561.1 50.3 %while.49 = (s32[]{:T(128)}, f32[128,1,4]{0,2,1:T(4,128)S(1)}, f32[128,1,4]{0,2,1:T(4,128)S(1)}, f32[128,1,4,128]{3,2,1,0:T(4,128)S(1)}, f32[15,128,1,4]{1,3,2,0...) while((s32[]{:T(128)}, f32[128,1,4]{0,2,1:T(4,128)S(1)}, ...), condition=%wide.region_22.23_spmd, body=%wide.region_21.22_spmd.sunk | while | flops 200194 | bytes 825441 | solution.py:19
  616.5 50.3 %while.48 = (s32[]{:T(128)}, f32[128,1,4]{0,2,1:T(4,128)S(1)}, f32[128,1,4]{0,2,1:T(4,128)S(1)}, f32[128,1,4,128]{3,2,1,0:T(4,128)S(1)}, f32[15,128,1,4]{1,3,2,0...) while((s32[]{:T(128)}, f32[128,1,4]{0,2,1:T(4,128)S(1)}, ...), condition=%wide.region_15.16_spmd, body=%wide.region_14.15_spmd.sunk | while | flops 200194 | bytes 825441 | solution.py:19
  (550 shorter events, 534.9 us)
Async XLA Ops:
  7.2 549.4 %all-gather.11.cloned.1.call-start = ((), (), s32[]{:S(2)}) async-start(), calls=%async_computation.1 | async-start | bytes 4456448 | tf_op jit(solution)/shard_map/all_gather | solution.py:16
  28.0 129.6 %copy-start.21 = (bf16[2,8,128]{2,1,0:T(8,128)(2,1)S(1)}, bf16[2,8,128]{2,1,0:T(8,128)(2,1)}, u32[]{:S(2)}) copy-start(bf16[2,8,128]{2,1,0:T(8,128)(2,1)} %param.22) | copy-start | bytes 12292
  30.1 131.5 %copy-start.20 = (bf16[2,8,128]{2,1,0:T(8,128)(2,1)S(1)}, bf16[2,8,128]{2,1,0:T(8,128)(2,1)}, u32[]{:S(2)}) copy-start(bf16[2,8,128]{2,1,0:T(8,128)(2,1)} %param.23) | copy-start | bytes 12292
  34.7 129.7 %copy-start.10 = (bf16[1024,128]{1,0:T(8,128)(2,1)S(1)}, bf16[1024,128]{1,0:T(8,128)(2,1)}, u32[]{:S(2)}) copy-start(bf16[1024,128]{1,0:T(8,128)(2,1)} %param.19) | copy-start | bytes 786436
  50.4 561.6 %all-gather.9.cloned.1.call-start = ((), (), s32[]{:S(2)}) async-start(), calls=%async_computation | async-start | bytes 4456448 | tf_op jit(solution)/shard_map/all_gather | solution.py:16
  184.8 376.3 %copy-start.7 = (f32[128,1,4]{0,2,1:T(4,128)S(1)}, f32[128,1,4]{0,2,1:T(4,128)}, u32[]{:S(2)}) copy-start(f32[128,1,4]{0,2,1:T(4,128)} %slice_bitcast_fusion.8) | copy-start | bytes 6148
  184.8 376.3 %copy-start.13 = (f32[128,1,4]{0,2,1:T(4,128)S(1)}, f32[128,1,4]{0,2,1:T(4,128)}, u32[]{:S(2)}) copy-start(f32[128,1,4]{0,2,1:T(4,128)} %copy.189) | copy-start | bytes 6148
  185.1 3.8 collective-permute-start
  202.8 10.1 %collective-permute-start = (bf16[2,1024,128]{2,1,0:T(8,128)(2,1)S(1)}, bf16[2,1024,128]{2,1,0:T(8,128)(2,1)S(1)}, u32[]{:S(2)}, u32[]{:S(2)}) collective-permute-start(bf16[2,1024,128]{2,1,0:T(8,128)(2,1)S(1)} %get-tuple-element.711), channel_id=1, source_target_pairs={{0,8},{8,16},{16,24},{24,32},{32,40},{40,48},{48,56},{56,64},{64,7... | collective-permute-start | bytes 1572872 | tf_op jit(solution)/shard_map/while/body/eval_jaxpr/ppermute | solution.py:12
  226.8 10.5 %collective-permute-start = (bf16[2,1024,128]{2,1,0:T(8,128)(2,1)S(1)}, bf16[2,1024,128]{2,1,0:T(8,128)(2,1)S(1)}, u32[]{:S(2)}, u32[]{:S(2)}) collective-permute-start(bf16[2,1024,128]{2,1,0:T(8,128)(2,1)S(1)} %get-tuple-element.711), channel_id=1, source_target_pairs={{0,8},{8,16},{16,24},{24,32},{32,40},{40,48},{48,56},{56,64},{64,7... | collective-permute-start | bytes 1572872 | tf_op jit(solution)/shard_map/while/body/eval_jaxpr/ppermute | solution.py:12
  251.2 10.5 %collective-permute-start = (bf16[2,1024,128]{2,1,0:T(8,128)(2,1)S(1)}, bf16[2,1024,128]{2,1,0:T(8,128)(2,1)S(1)}, u32[]{:S(2)}, u32[]{:S(2)}) collective-permute-start(bf16[2,1024,128]{2,1,0:T(8,128)(2,1)S(1)} %get-tuple-element.711), channel_id=1, source_target_pairs={{0,8},{8,16},{16,24},{24,32},{32,40},{40,48},{48,56},{56,64},{64,7... | collective-permute-start | bytes 1572872 | tf_op jit(solution)/shard_map/while/body/eval_jaxpr/ppermute | solution.py:12
  275.6 10.5 %collective-permute-start = (bf16[2,1024,128]{2,1,0:T(8,128)(2,1)S(1)}, bf16[2,1024,128]{2,1,0:T(8,128)(2,1)S(1)}, u32[]{:S(2)}, u32[]{:S(2)}) collective-permute-start(bf16[2,1024,128]{2,1,0:T(8,128)(2,1)S(1)} %get-tuple-element.711), channel_id=1, source_target_pairs={{0,8},{8,16},{16,24},{24,32},{32,40},{40,48},{48,56},{56,64},{64,7... | collective-permute-start | bytes 1572872 | tf_op jit(solution)/shard_map/while/body/eval_jaxpr/ppermute | solution.py:12
  300.0 10.5 %collective-permute-start = (bf16[2,1024,128]{2,1,0:T(8,128)(2,1)S(1)}, bf16[2,1024,128]{2,1,0:T(8,128)(2,1)S(1)}, u32[]{:S(2)}, u32[]{:S(2)}) collective-permute-start(bf16[2,1024,128]{2,1,0:T(8,128)(2,1)S(1)} %get-tuple-element.711), channel_id=1, source_target_pairs={{0,8},{8,16},{16,24},{24,32},{32,40},{40,48},{48,56},{56,64},{64,7... | collective-permute-start | bytes 1572872 | tf_op jit(solution)/shard_map/while/body/eval_jaxpr/ppermute | solution.py:12
  324.4 10.5 %collective-permute-start = (bf16[2,1024,128]{2,1,0:T(8,128)(2,1)S(1)}, bf16[2,1024,128]{2,1,0:T(8,128)(2,1)S(1)}, u32[]{:S(2)}, u32[]{:S(2)}) collective-permute-start(bf16[2,1024,128]{2,1,0:T(8,128)(2,1)S(1)} %get-tuple-element.711), channel_id=1, source_target_pairs={{0,8},{8,16},{16,24},{24,32},{32,40},{40,48},{48,56},{56,64},{64,7... | collective-permute-start | bytes 1572872 | tf_op jit(solution)/shard_map/while/body/eval_jaxpr/ppermute | solution.py:12
  348.8 10.5 %collective-permute-start = (bf16[2,1024,128]{2,1,0:T(8,128)(2,1)S(1)}, bf16[2,1024,128]{2,1,0:T(8,128)(2,1)S(1)}, u32[]{:S(2)}, u32[]{:S(2)}) collective-permute-start(bf16[2,1024,128]{2,1,0:T(8,128)(2,1)S(1)} %get-tuple-element.711), channel_id=1, source_target_pairs={{0,8},{8,16},{16,24},{24,32},{32,40},{40,48},{48,56},{56,64},{64,7... | collective-permute-start | bytes 1572872 | tf_op jit(solution)/shard_map/while/body/eval_jaxpr/ppermute | solution.py:12
  373.1 10.5 %collective-permute-start = (bf16[2,1024,128]{2,1,0:T(8,128)(2,1)S(1)}, bf16[2,1024,128]{2,1,0:T(8,128)(2,1)S(1)}, u32[]{:S(2)}, u32[]{:S(2)}) collective-permute-start(bf16[2,1024,128]{2,1,0:T(8,128)(2,1)S(1)} %get-tuple-element.711), channel_id=1, source_target_pairs={{0,8},{8,16},{16,24},{24,32},{32,40},{40,48},{48,56},{56,64},{64,7... | collective-permute-start | bytes 1572872 | tf_op jit(solution)/shard_map/while/body/eval_jaxpr/ppermute | solution.py:12
  397.5 10.5 %collective-permute-start = (bf16[2,1024,128]{2,1,0:T(8,128)(2,1)S(1)}, bf16[2,1024,128]{2,1,0:T(8,128)(2,1)S(1)}, u32[]{:S(2)}, u32[]{:S(2)}) collective-permute-start(bf16[2,1024,128]{2,1,0:T(8,128)(2,1)S(1)} %get-tuple-element.711), channel_id=1, source_target_pairs={{0,8},{8,16},{16,24},{24,32},{32,40},{40,48},{48,56},{56,64},{64,7... | collective-permute-start | bytes 1572872 | tf_op jit(solution)/shard_map/while/body/eval_jaxpr/ppermute | solution.py:12
  421.9 10.5 %collective-permute-start = (bf16[2,1024,128]{2,1,0:T(8,128)(2,1)S(1)}, bf16[2,1024,128]{2,1,0:T(8,128)(2,1)S(1)}, u32[]{:S(2)}, u32[]{:S(2)}) collective-permute-start(bf16[2,1024,128]{2,1,0:T(8,128)(2,1)S(1)} %get-tuple-element.711), channel_id=1, source_target_pairs={{0,8},{8,16},{16,24},{24,32},{32,40},{40,48},{48,56},{56,64},{64,7... | collective-permute-start | bytes 1572872 | tf_op jit(solution)/shard_map/while/body/eval_jaxpr/ppermute | solution.py:12
  446.3 10.5 %collective-permute-start = (bf16[2,1024,128]{2,1,0:T(8,128)(2,1)S(1)}, bf16[2,1024,128]{2,1,0:T(8,128)(2,1)S(1)}, u32[]{:S(2)}, u32[]{:S(2)}) collective-permute-start(bf16[2,1024,128]{2,1,0:T(8,128)(2,1)S(1)} %get-tuple-element.711), channel_id=1, source_target_pairs={{0,8},{8,16},{16,24},{24,32},{32,40},{40,48},{48,56},{56,64},{64,7... | collective-permute-start | bytes 1572872 | tf_op jit(solution)/shard_map/while/body/eval_jaxpr/ppermute | solution.py:12
  470.7 11.7 %collective-permute-start = (bf16[2,1024,128]{2,1,0:T(8,128)(2,1)S(1)}, bf16[2,1024,128]{2,1,0:T(8,128)(2,1)S(1)}, u32[]{:S(2)}, u32[]{:S(2)}) collective-permute-start(bf16[2,1024,128]{2,1,0:T(8,128)(2,1)S(1)} %get-tuple-element.711), channel_id=1, source_target_pairs={{0,8},{8,16},{16,24},{24,32},{32,40},{40,48},{48,56},{56,64},{64,7... | collective-permute-start | bytes 1572872 | tf_op jit(solution)/shard_map/while/body/eval_jaxpr/ppermute | solution.py:12
  496.3 14.1 %collective-permute-start = (bf16[2,1024,128]{2,1,0:T(8,128)(2,1)S(1)}, bf16[2,1024,128]{2,1,0:T(8,128)(2,1)S(1)}, u32[]{:S(2)}, u32[]{:S(2)}) collective-permute-start(bf16[2,1024,128]{2,1,0:T(8,128)(2,1)S(1)} %get-tuple-element.711), channel_id=1, source_target_pairs={{0,8},{8,16},{16,24},{24,32},{32,40},{40,48},{48,56},{56,64},{64,7... | collective-permute-start | bytes 1572872 | tf_op jit(solution)/shard_map/while/body/eval_jaxpr/ppermute | solution.py:12
  524.3 14.1 %collective-permute-start = (bf16[2,1024,128]{2,1,0:T(8,128)(2,1)S(1)}, bf16[2,1024,128]{2,1,0:T(8,128)(2,1)S(1)}, u32[]{:S(2)}, u32[]{:S(2)}) collective-permute-start(bf16[2,1024,128]{2,1,0:T(8,128)(2,1)S(1)} %get-tuple-element.711), channel_id=1, source_target_pairs={{0,8},{8,16},{16,24},{24,32},{32,40},{40,48},{48,56},{56,64},{64,7... | collective-permute-start | bytes 1572872 | tf_op jit(solution)/shard_map/while/body/eval_jaxpr/ppermute | solution.py:12
  552.4 115.6 %copy-start.1 = (s32[128]{0:T(128)S(1)}, s32[128]{0:T(128)}, u32[]{:S(2)}) copy-start(s32[128]{0:T(128)} %param.27) | copy-start | bytes 1540
  554.6 112.5 %copy-start.16 = (f32[8,128]{1,0:T(8,128)S(1)}, f32[8,128]{1,0:T(8,128)}, u32[]{:S(2)}) copy-start(f32[8,128]{1,0:T(8,128)} %get-tuple-element.518) | copy-start | bytes 12292
  (43 other events, 740.3 us)
Sparse Core Ops, SparseCore 0:
  50.6 57.5 all-gather.10
  110.6 57.3 all-gather.8
where the time goes:
time: 678 us; the launch traced here: 675 us
  other arithmetic  188 us (28%)
  matrix products  163 us (24%)
  waiting for transfers between devices  139 us (21%)
  blocking collectives  110 us (16%)
  local copies, waits for them, and re-layouts  37.5 us (6%)
  starting transfers between devices  19.5 us (3%)
  between operations  14.6 us (2%)
    ppermute x15, waiting for transfers between devices, shifted(): lax.ppermute(value, axis, [(source, source + steps) for source in range(l...  139 us
    dot_general x16, matrix products, attend(): jnp.einsum('tkgs,skd->tkgd', weights.astype(jnp.bfloat16), value_rows, pr...  93.8 us
    all_gather x4, blocking collectives, combined_all(): pieces = jax.tree.map(lambda part: lax.all_gather(part, axis), value)  90.3 us
    reduce_sum x16, other arithmetic, attend(): run_sum = run_sum * factor + jnp.sum(weights, axis=-1)  67 us
    dot_general x16, matrix products, attend(): jnp.einsum('tkgd,skd->tkgs', queries, key_rows, preferred_element_type=jn...  52.8 us
    add x30, other arithmetic, combine_parts(): out_a * factor_a[..., None] + out_b * factor_b[..., None]  52.5 us
    mul x31, other arithmetic, combine_parts(): out_b * factor_b[..., None]  20.8 us
    mul x32, other arithmetic, combine_parts(): out_a * factor_a[..., None] + out_b * factor_b[..., None]  20 us
  transfers between devices with their start and end apart: 17, of which 15 were waited for; matrix products, arithmetic and copies ran while one was open for 46% of the time, Pallas kernels for 0%

commit v1 on v0

v1 whole, which is shorter than its diff:
```python
import functools
import math

import jax
import jax.numpy as jnp
from jax import lax
from jax.experimental import pallas as pl
from jax.experimental.pallas import tpu as pltpu
from jax.sharding import PartitionSpec as P

HD = 128
SCALE2 = HD**-0.5 * math.log2(math.e)
LOW = -1e30
HEADS = 4
ROWS = 512
KEYS = 1024
CHUNK = 256
SLOTS = 8
VMEM = pl.BlockSpec(memory_space=pltpu.VMEM)
SMEM = pl.BlockSpec(memory_space=pltpu.SMEM)
ANY = pl.BlockSpec(memory_space=pl.ANY)
NT = (((1,), (1,)), ((), ()))


def index_of(z, y, c):
    return (z % 2) * 8 + (y % 4) * 2 + c % 2


def moves(dz, dy, dc):
    return [
        (index_of(z, y, c), index_of(z + dz, y + dy, c + dc))
        for z in range(2)
        for y in range(4)
        for c in range(2)
    ]


def permute(value, pairs):
    return lax.ppermute(value, "inst", pairs)


def flash_kernel(half_count, sources, has_state, final, diag, *refs):
    refs = list(refs)
    meta, q_ref = refs.pop(0), refs.pop(0)
    kv_refs = [refs.pop(0) for _ in range(1 + max(src for src, *_ in sources))]
    state_in = [refs.pop(0) for _ in range(2)] if has_state else None
    outs = [refs.pop(0) for _ in range(1 if final else 2)]
    kv, qs, acc, top, scores, row_top, items, sem = refs

    copies = [
        pltpu.make_async_copy(
            kv_refs[src].at[pl.ds(first, count)],
            kv.at[slot, pl.ds(row, count)],
            sem.at[k],
        )
        for k, (src, first, count, slot, row) in enumerate(sources)
    ]
    for copy in copies:
        copy.start()

    for half in range(half_count):
        for h in range(HEADS):
            scaled = q_ref[half, :, h * HD : (h + 1) * HD].astype(jnp.float32) * SCALE2
            high = scaled.astype(jnp.bfloat16)
            qs[half, h, :, :HD] = high
            qs[half, h, :, HD:] = (scaled - high.astype(jnp.float32)).astype(jnp.bfloat16)
    if has_state:
        lane = lax.broadcasted_iota(jnp.int32, (ROWS, HD), 1)
        for half in range(half_count):
            for h in range(HEADS):
                acc[half, h, :, :HD] = state_in[0][half, h]
                stat = state_in[1][half, h]
                top[half, h] = jnp.broadcast_to(stat[:, :1], (ROWS, HD))
                acc[half, h, :, HD:] = jnp.broadcast_to(stat[:, HD - 1 :], (ROWS, HD))
    else:
        acc[...] = jnp.zeros_like(acc)
        top[...] = jnp.full_like(top, LOW)

    count = jnp.int32(0)
    for half in range(half_count):
        limit = meta[SLOTS + half]
        for slot in range(SLOTS):
            wanted = meta[slot] < limit

            @pl.when(wanted)
            def _(count=count, half=half, slot=slot):
                items[count] = half * SLOTS + slot

            count = count + wanted.astype(jnp.int32)

    for copy in copies:
        copy.wait()

    ones = jnp.ones((KEYS, HD), jnp.bfloat16)

    def update(half, h, row, s, new_top, values):
        old_top = top[half, h, pl.ds(row, CHUNK), :]
        new_top = jnp.maximum(old_top, new_top)
        factor = jnp.exp2(old_top - new_top)
        weights = jnp.exp2(s - new_top[:, :1])
        top[half, h, pl.ds(row, CHUNK), :] = new_top
        mixed = jnp.dot(
            weights.astype(jnp.bfloat16),
            jnp.concatenate([values, ones[: values.shape[0]]], axis=1),
            preferred_element_type=jnp.float32,
        )
        for part in range(2):
            cols = slice(part * HD, (part + 1) * HD)
            acc[half, h, pl.ds(row, CHUNK), cols] = (
                acc[half, h, pl.ds(row, CHUNK), cols] * factor + mixed[:, cols]
            )

    if diag is not None:
        half, first_row = diag
        slot = meta[SLOTS + half_count]
        for r in range(ROWS // CHUNK):
            seen = first_row + (r + 1) * CHUNK
            key_rows = kv[slot, :seen, :HD]
            key_rows = jnp.concatenate([key_rows, key_rows], axis=1)
            row_pos = lax.broadcasted_iota(jnp.int32, (CHUNK, seen), 0) + (seen - CHUNK)
            allowed = lax.broadcasted_iota(jnp.int32, (CHUNK, seen), 1) <= row_pos
            for h in range(HEADS):
                s = lax.dot_general(
                    qs[half, h, r * CHUNK : (r + 1) * CHUNK, :],
                    key_rows,
                    NT,
                    preferred_element_type=jnp.float32,
                )
                s = jnp.where(allowed, s, LOW)
                update(
                    half, h, r * CHUNK, s, jnp.max(s, axis=-1, keepdims=True), kv[slot, :seen, HD:]
                )

    def place(item):
        code = items[item]
        return code // SLOTS, code % SLOTS

    def produce(item, r):
        half, slot = place(item)
        key_rows = kv[slot, :, :HD]
        key_rows = jnp.concatenate([key_rows, key_rows], axis=1)
        for h in range(HEADS):
            s = lax.dot_general(
                qs[half, h, r * CHUNK : (r + 1) * CHUNK, :],
                key_rows,
                NT,
                preferred_element_type=jnp.float32,
            )
            scores[r, h] = s
            row_top[r, h] = jnp.broadcast_to(jnp.max(s, axis=-1, keepdims=True), (CHUNK, HD))

    def consume(item, r):
        half, slot = place(item)
        for h in range(HEADS):
            update(half, h, r * CHUNK, scores[r, h], row_top[r, h], kv[slot, :, HD:])

    @pl.when(count > 0)
    def _():
        produce(0, 0)

        @pl.loop(0, count)
        def _(item):
            produce(item, 1)
            consume(item, 0)
            produce(jnp.minimum(item + 1, count - 1), 0)
            consume(item, 1)

    for half in range(half_count):
        for h in range(HEADS):
            if final:
                outs[0][half, :, h * HD : (h + 1) * HD] = (
                    acc[half, h, :, :HD] / acc[half, h, :, HD:]
                ).astype(jnp.bfloat16)
            else:
                lane = lax.broadcasted_iota(jnp.int32, (ROWS, HD), 1)
                outs[0][half, h] = acc[half, h, :, :HD]
                outs[1][half, h] = jnp.where(lane < HD // 2, top[half, h], acc[half, h, :, HD:])


def flash(meta, queries, kv_arrays, sources, state=None, final=False, diag=None):
    half_count = queries.shape[0]
    if final:
        out_shape = [jax.ShapeDtypeStruct((half_count, ROWS, HEADS * HD), jnp.bfloat16)]
    else:
        out_shape = [jax.ShapeDtypeStruct((half_count, HEADS, ROWS, HD), jnp.float32)] * 2
    operands = [meta, queries, *kv_arrays, *(state or [])]
    in_specs = [SMEM, VMEM] + [ANY] * len(kv_arrays) + [VMEM] * (2 if state else 0)
    work = half_count * SLOTS * HEADS * ROWS * KEYS // 2
    return pl.pallas_call(
        functools.partial(flash_kernel, half_count, sources, state is not None, final, diag),
        out_shape=out_shape,
        in_specs=in_specs,
        out_specs=[VMEM] * len(out_shape),
        scratch_shapes=[
            pltpu.VMEM((SLOTS, KEYS, 2 * HD), jnp.bfloat16),
            pltpu.VMEM((half_count, HEADS, ROWS, 2 * HD), jnp.bfloat16),
            pltpu.VMEM((half_count, HEADS, ROWS, 2 * HD), jnp.float32),
            pltpu.VMEM((half_count, HEADS, ROWS, HD), jnp.float32),
            pltpu.VMEM((2, HEADS, CHUNK, KEYS), jnp.float32),
            pltpu.VMEM((2, HEADS, CHUNK, HD), jnp.float32),
            pltpu.SMEM((2 * SLOTS,), jnp.int32),
            pltpu.SemaphoreType.DMA((len(sources),)),
        ],
        compiler_params=pltpu.CompilerParams(vmem_limit_bytes=48 << 20),
        cost_estimate=pl.CostEstimate(
            flops=work * HD * 4 * 2, bytes_accessed=16 << 20, transcendentals=work
        ),
    )(*operands)


GROUP = 16
QROWS = 8


def decode_kernel(owner, live, q_ref, k_ref, v_ref, out_ref, spread, top, total, mixed):
    step = pl.program_id(0)

    @pl.when(step == 0)
    def _():
        spread[...] = jnp.zeros_like(spread)
        top[...] = jnp.full_like(top, LOW)
        total[...] = jnp.zeros_like(total)
        mixed[...] = jnp.zeros_like(mixed)

    zero = jnp.zeros((QROWS, HD), jnp.float32)
    reqs = [owner[step * GROUP + b] for b in range(GROUP)]
    for b in range(0, GROUP, 2):
        pair = jnp.concatenate(
            [
                jnp.concatenate([q_ref[reqs[b]], zero], axis=1),
                jnp.concatenate([zero, q_ref[reqs[b + 1]]], axis=1),
            ],
            axis=0,
        )
        spread[b * QROWS : (b + 2) * QROWS, b * HD : (b + 2) * HD] = pair.astype(jnp.bfloat16)
    keys = jnp.concatenate([k_ref[b] for b in range(GROUP)], axis=1)
    values = jnp.concatenate([v_ref[b] for b in range(GROUP)], axis=1)
    scores = lax.dot_general(spread[...], keys, NT, preferred_element_type=jnp.float32) * SCALE2
    slot_pos = lax.broadcasted_iota(jnp.int32, (QROWS, HD), 1)
    block_top, weights = [], []
    for b in range(GROUP):
        alive = slot_pos < live[step * GROUP + b]
        s = jnp.where(alive, scores[b * QROWS : (b + 1) * QROWS], LOW)
        highest = jnp.max(s, axis=-1, keepdims=True)
        block_top.append(jnp.broadcast_to(highest, (QROWS, HD)))
        weights.append(jnp.where(alive, jnp.exp2(s - highest), 0.0))
    result = jnp.dot(
        jnp.concatenate(weights, axis=0).astype(jnp.bfloat16),
        values,
        preferred_element_type=jnp.float32,
    )
    for b in range(GROUP):
        r = reqs[b]
        part = result[b * QROWS : (b + 1) * QROWS, b * HD : (b + 1) * HD]
        part_sum = jnp.sum(weights[b], axis=-1, keepdims=True)
        old_top = top[r]
        new_top = jnp.maximum(old_top, block_top[b])
        old_factor = jnp.exp2(old_top - new_top)
        new_factor = jnp.exp2(block_top[b] - new_top)
        top[r] = new_top
        total[r] = total[r] * old_factor + part_sum * new_factor
        mixed[r] = mixed[r] * old_factor + part * new_factor

    @pl.when(step == pl.num_programs(0) - 1)
    def _():
        sums = total[...]
        held = sums > 0.0
        safe = jnp.where(held, sums, 1.0)
        level = jnp.where(held, top[...] + jnp.log2(safe), LOW)
        first = level.astype(jnp.bfloat16).astype(jnp.float32)
        second = (level - first).astype(jnp.bfloat16).astype(jnp.float32)
        third = level - first - second
        lane = lax.broadcasted_iota(jnp.int32, level.shape, 2)
        terms = jnp.where(lane == 0, first, jnp.where(lane == 1, second, third))
        out_ref[...] = jnp.concatenate([mixed[...] / safe, terms], axis=1).astype(jnp.bfloat16)


def decode_cache(owner, live, queries, k_cache, v_cache):
    req_count, block_count = queries.shape[0], k_cache.shape[0]
    state = pltpu.VMEM((req_count, QROWS, HD), jnp.float32)
    return pl.pallas_call(
        decode_kernel,
        out_shape=jax.ShapeDtypeStruct((req_count, 2 * QROWS, HD), jnp.bfloat16),
        grid_spec=pltpu.PrefetchScalarGridSpec(
            num_scalar_prefetch=2,
            grid=(block_count // GROUP,),
            in_specs=[
                pl.BlockSpec((req_count, QROWS, HD), lambda i, *_: (0, 0, 0)),
                pl.BlockSpec((GROUP, HD, HD), lambda i, *_: (i, 0, 0)),
                pl.BlockSpec((GROUP, HD, HD), lambda i, *_: (i, 0, 0)),
            ],
            out_specs=pl.BlockSpec((req_count, 2 * QROWS, HD), lambda i, *_: (0, 0, 0)),
            scratch_shapes=[pltpu.VMEM((GROUP * QROWS, GROUP * HD), jnp.bfloat16), state, state, state],
        ),
        compiler_params=pltpu.CompilerParams(
            dimension_semantics=("arbitrary",), vmem_limit_bytes=32 << 20
        ),
        cost_estimate=pl.CostEstimate(
            flops=1 << 32, bytes_accessed=9 << 20, transcendentals=1 << 20
        ),
    )(owner, live, queries, k_cache, v_cache)


def merge_kernel(parts_ref, q_ref, k_ref, v_ref, out_ref):
    source_count, req_count = parts_ref.shape[0], parts_ref.shape[1]
    for r in range(req_count):
        queries = q_ref[r]
        row = lax.broadcasted_iota(jnp.int32, (QROWS, 1), 0)
        levels, pieces = [], []
        for s in range(source_count):
            both = parts_ref[s, r].astype(jnp.float32)
            terms = both[QROWS:]
            levels.append(terms[:, 0:1] + terms[:, 1:2] + terms[:, 2:3])
            pieces.append(both[:QROWS])
        for n in range(2):
            key = k_ref[n, r : r + 1, :]
            score = jnp.sum(queries * key, axis=-1, keepdims=True) * SCALE2
            if n:
                score = jnp.where(row >= n * HEADS, score, LOW)
            levels.append(score)
            pieces.append(jnp.broadcast_to(v_ref[n, r : r + 1, :], (QROWS, HD)))
        highest = functools.reduce(jnp.maximum, levels)
        shares = [jnp.exp2(level - highest) for level in levels]
        result = functools.reduce(jnp.add, [w * p for w, p in zip(shares, pieces)])
        out_ref[r] = result / functools.reduce(jnp.add, shares)


def decode_merge(parts, queries, k_new, v_new):
    return pl.pallas_call(
        merge_kernel,
        out_shape=jax.ShapeDtypeStruct(queries.shape, jnp.float32),
        in_specs=[VMEM] * 4,
        out_specs=VMEM,
    )(parts, queries, k_new.astype(jnp.float32), v_new.astype(jnp.float32))


def body(
    q_prefill,
    k_prefill,
    v_prefill,
    q_decode,
    k_new,
    v_new,
    k_cache,
    v_cache,
    block_table,
    req_lengths,
):
    me = lax.axis_index("inst")
    z, y, c = me // 8, (me // 2) % 4, me % 2
    steps, req_local, _ = q_decode.shape

    own_queries = q_decode.reshape(steps, req_local, HEADS, HD).transpose(1, 0, 2, 3)
    own_queries = own_queries.reshape(req_local, QROWS, HD)
    every_query = lax.all_gather(own_queries, "inst", axis=0, tiled=True)

    own = jnp.concatenate([k_prefill, v_prefill], axis=1)
    up = permute(own, moves(0, 1, 0))
    down = permute(own, moves(0, -1, 0))
    across = permute(own, moves(1, 0, 0))
    beside = permute(own, moves(0, 0, 1))
    mirror = [(i, 15 - i) for i in range(16)]
    other_rows = permute(q_prefill[ROWS:], mirror)
    queries = jnp.stack([q_prefill[:ROWS], other_rows])

    up_more = permute(jnp.concatenate([across, up[:ROWS]]), moves(0, 1, 0))
    down_more = permute(jnp.concatenate([across, down[ROWS:]]), moves(0, -1, 0))
    beside_near = permute(jnp.concatenate([up, down, across]), moves(0, 0, 1))

    limits = jnp.stack([me, 15 - me])
    near_ids = [
        me,
        index_of(z, y, c + 1),
        index_of(z, y + 3, c),
        index_of(z, y + 1, c),
        index_of(z + 1, y, c),
        index_of(z, y + 3, c + 1),
        index_of(z, y + 1, c + 1),
        index_of(z + 1, y, c + 1),
    ]
    near_meta = jnp.concatenate([jnp.stack(near_ids), limits, jnp.zeros((1,), jnp.int32)])
    near_sources = [(k, 0, KEYS, k, 0) for k in range(5)]
    near_sources += [(5, k * KEYS, KEYS, 5 + k, 0) for k in range(3)]
    state = flash(
        near_meta.astype(jnp.int32),
        queries,
        [own, beside, up, down, across, beside_near],
        near_sources,
        diag=(0, 0),
    )

    up_last = permute(up_more[:ROWS], moves(0, 1, 0))
    down_last = permute(down_more[ROWS:KEYS], moves(0, -1, 0))
    beside_far = permute(jnp.concatenate([up_more, down_more]), moves(0, 0, 1))
    beside_last = permute(jnp.concatenate([up_last, down_last]), moves(0, 0, 1))
    far_ids = [
        index_of(z, y + 2, c),
        index_of(z + 1, y + 3, c),
        index_of(z + 1, y + 1, c),
        index_of(z + 1, y + 2, c),
        index_of(z, y + 2, c + 1),
        index_of(z + 1, y + 3, c + 1),
        index_of(z + 1, y + 1, c + 1),
        index_of(z + 1, y + 2, c + 1),
    ]
    far_arrays = [up_more, down_more, up_last, down_last, beside_far, beside_last]
    both = KEYS + ROWS
    far_sources = [
        (0, KEYS, ROWS, 0, 0),
        (1, KEYS, ROWS, 0, ROWS),
        (0, 0, KEYS, 1, 0),
        (1, 0, KEYS, 2, 0),
        (2, 0, ROWS, 3, 0),
        (3, 0, ROWS, 3, ROWS),
        (4, KEYS, ROWS, 4, 0),
        (4, both + KEYS, ROWS, 4, ROWS),
        (4, 0, KEYS, 5, 0),
        (4, both, KEYS, 6, 0),
        (5, 0, KEYS, 7, 0),
    ]
    mirror_slot = jnp.where(y % 2 == 0, 5, 6)
    far_ids = jnp.stack(far_ids)
    other_meta = jnp.concatenate([far_ids, limits[1:], mirror_slot[None]]).astype(jnp.int32)
    own_meta = jnp.concatenate([far_ids, limits[:1], mirror_slot[None]]).astype(jnp.int32)
    (other_out,) = flash(
        other_meta,
        queries[1:],
        far_arrays,
        far_sources,
        state=[part[1:] for part in state],
        final=True,
        diag=(0, ROWS),
    )
    last_rows = permute(other_out[0], mirror)
    (own_out,) = flash(
        own_meta,
        queries[:1],
        far_arrays,
        far_sources,
        state=[part[:1] for part in state],
        final=True,
    )

    block_count, block_len = k_cache.shape[:2]
    width = block_table.shape[1]
    global_id = me * block_count + jnp.arange(block_count, dtype=jnp.int32)
    matches = block_table.reshape(-1)[None, :] == global_id[:, None]
    place = jnp.arange(block_table.size, dtype=jnp.int32)[None, :]
    flat = jnp.sum(jnp.where(matches, place, 0), axis=1)
    owner = flat // width
    left = req_lengths[:, None] - jnp.arange(width, dtype=jnp.int32)[None, :] * block_len
    left = jnp.clip(left, 0, block_len).reshape(-1)
    live = jnp.sum(jnp.where(matches, left[None, :], 0), axis=1)
    parts = decode_cache(owner, live, every_query.astype(jnp.float32), k_cache, v_cache)
    parts = lax.all_to_all(parts, "inst", 0, 0, tiled=True)
    parts = parts.reshape(-1, req_local, 2 * QROWS, HD)
    result = decode_merge(parts, own_queries.astype(jnp.float32), k_new, v_new)
    result = result.astype(jnp.bfloat16).reshape(req_local, steps, HEADS * HD)
    decode_out = result.transpose(1, 0, 2)

    prefill_out = jnp.concatenate([own_out[0], last_rows])
    return prefill_out, decode_out


def solution(mesh):
    placed = (
        P("inst", "tp"),
        P("inst", "tp"),
        P("inst", "tp"),
        P(None, "inst", "tp"),
        P(None, "inst", "tp"),
        P(None, "inst", "tp"),
        P("inst", None, "tp"),
        P("inst", None, "tp"),
        P(),
        P(),
    )
    return jax.shard_map(
        body,
        mesh=mesh,
        in_specs=placed,
        out_specs=(P("inst", "tp"), P(None, "inst", "tp")),
        check_vma=False,
    )
```

time: 678 us -> 181 us (0.27)
  the two profiles are of different devices: /device:TPU:121 before, /device:TPU:127 now
where the time goes in v1:
time: 181 us; the launch traced here: 180 us
  Pallas kernels  65.7 us (36%)
  starting transfers between devices  48.3 us (27%)
  blocking collectives  31.7 us (18%)
  waiting for transfers between devices  12.9 us (7%)
  local copies, waits for them, and re-layouts  12.1 us (7%)
  other arithmetic  8.75 us (5%)
    pallas_call x3, Pallas kernels, flash(): pl.pallas_call(functools.partial(flash_kernel, half_count, sources, state...  55.5 us
    ppermute x13, starting transfers between devices, permute(): return lax.ppermute(value, 'inst', pairs)  38.2 us
    all_gather x1, blocking collectives, body(): every_query = lax.all_gather(own_queries, 'inst', axis=0, tiled=True)  31.7 us
    all_to_all x1, starting transfers between devices, body(): parts = lax.all_to_all(parts, 'inst', 0, 0, tiled=True)  10.1 us
    pallas_call x1, Pallas kernels, decode_cache(): pl.pallas_call(decode_kernel, out_shape=jax.ShapeDtypeStruct((req_count,...  7.93 us
    ppermute x13, waiting for transfers between devices, permute(): return lax.ppermute(value, 'inst', pairs)  7.49 us
    all_to_all x1, waiting for transfers between devices, body(): parts = lax.all_to_all(parts, 'inst', 0, 0, tiled=True)  5.44 us
    unnamed x30, local copies, waits for them, and re-layouts  5.32 us
  transfers between devices with their start and end apart: 14, of which 3 were waited for; matrix products, arithmetic and copies ran while one was open for 8% of the time, Pallas kernels for 33%

profile of v1, /device:TPU:127, one launch (start us, length us, event | category | flops | bytes accessed | tf_op | source)
XLA Modules:
  0.0 180.5 jit_solution(10321851846578887361)
XLA Ops:
  3.1 1.5 collective-permute-start.3
  4.5 2.1 %slice_bitcast_fusion = (bf16[1,512,512]{2,1,0:T(8,128)(2,1)S(1)}, bf16[512,512]{1,0:T(8,128)(2,1)}) fusion(bf16[1024,512]{1,0:T(8,128)(2,1)} %param.10), kind=kLoop, calls=%fused_computation.11 | loop fusion | bytes 2097152 | tf_op jit(solution)/shard_map/stack | solution.py:364
  6.6 5.0 %collective-permute-start.9 = (bf16[512,512]{1,0:T(8,128)(2,1)}, bf16[512,512]{1,0:T(8,128)(2,1)}, u32[]{:S(2)}, u32[]{:S(2)}) collective-permute-start(bf16[512,512]{1,0:T(8,128)(2,1)} %get-tuple-element.13), channel_id=1, source_target_pairs={{0,120},{8,112},{16,104},{24,96},{32,88},{40,80},{48,72},{56,64},{... | collective-permute-start | bytes 1572872 | tf_op jit(solution)/shard_map/ppermute | solution.py:39
  11.7 31.7 %all_gather.3 = bf16[128,8,128]{2,1,0:T(8,128)(2,1)S(1)} all-gather(bf16[8,8,128]{2,1,0:T(8,128)(2,1)S(1)} %bitcast.33), channel_id=1, replica_groups=mesh['inst'=16,'tp'=8] {'inst'}, dimensions={0}, use_global_device_ids=true | all-gather | bytes 278528 | tf_op jit(solution)/shard_map/all_gather | solution.py:355
  44.9 1.3 pad_maximum_fusion.1
  46.6 1.3 pad_maximum_fusion.4
  47.9 3.4 %collective-permute-start.2 = (bf16[1536,256]{1,0:T(8,128)(2,1)}, bf16[1536,256]{1,0:T(8,128)(2,1)S(1)}, u32[]{:S(2)}, u32[]{:S(2)}) collective-permute-start(bf16[1536,256]{1,0:T(8,128)(2,1)} %get-tuple-element.15), channel_id=1, source_target_pairs={{0,16},{8,24},{16,32},{24,40},{32,48},{40,56},{48,0},{56,8},{64,80... | collective-permute-start | bytes 2359304 | tf_op jit(solution)/shard_map/ppermute | solution.py:39
  51.4 2.2 %copy-done.7 = bf16[128,128,128]{2,1,0:T(8,128)(2,1)S(1)} copy-done((bf16[128,128,128]{2,1,0:T(8,128)(2,1)S(1)}, bf16[128,128,128]{2,1,0:T(8,128)(2,1)}, u32[]{:S(2)}) %copy-start.7) | copy-done | bytes 4194328
  53.6 7.9 %shard_map.116 = bf16[128,16,128]{2,1,0:T(8,128)(2,1)S(1)} custom-call(s32[128]{0:T(128)S(1)} %and_select_fusion.owner, s32[128]{0:T(128)S(1)} %get-tuple-element.6.live, f32[128,8,128]{2,1,0:T(8,128)S(1)} %copy-done.2, bf16[128,128,128]{2,1,0:T(8,128)(2,1)S(1)} %copy-done.6, bf16[128,128,128]{2,1,0:T(8,128)(2,1)S(1)} %copy-done.7), custom_call_target="tpu_custom_call" | custom-call | flops 4294967296 | bytes 9437184 | tf_op jit(solution)/shard_map/pallas_call | solution.py:281
  62.3 10.1 %all-to-all-start = ((bf16[128,16,128]{2,1,0:T(8,128)(2,1)}), bf16[128,16,128]{2,1,0:T(8,128)(2,1)}, u32[]{:S(2)}, u32[]{:S(2)}) async-start(bf16[128,16,128]{2,1,0:T(8,128)(2,1)} %copy-done.3), calls=%async_computation | async-start | bytes 1048576 | tf_op jit(solution)/shard_map/all_to_all | solution.py:455
  74.9 5.4 %all-to-all-done = bf16[128,16,128]{2,1,0:T(8,128)(2,1)} async-done(((bf16[128,16,128]{2,1,0:T(8,128)(2,1)}), bf16[128,16,128]{2,1,0:T(8,128)(2,1)}, u32[]{:S(2)}, u32[]{:S(2)}) %all-to-all-start) | async-done | bytes 524320 | tf_op jit(solution)/shard_map/all_to_all | solution.py:455
  80.3 2.3 %shard_map.117 = f32[8,8,128]{2,1,0:T(8,128)} custom-call(bf16[16,8,16,128]{3,2,1,0:T(8,128)(2,1)} %bitcast.25.parts_ref, f32[8,8,128]{2,1,0:T(8,128)} %convert_element_type.16.q_ref, f32[2,8,128]{2,1,0:T(8,128)} %convert_element_type.17.k_ref, f32[2,8,128]{2,1,0:T(8,128)} %convert_element_type.18.v_ref), custom_call_target="tpu_custom_call" | custom-call | tf_op jit(solution)/shard_map/pallas_call | solution.py:329
  84.1 1.1 pad_maximum_fusion.2.refs_1_
  85.3 1.9 %collective-permute-start.5 = (bf16[512,256]{1,0:T(8,128)(2,1)S(1)}, bf16[512,256]{1,0:T(8,128)(2,1)S(1)}, u32[]{:S(2)}, u32[]{:S(2)}) collective-permute-start(bf16[512,256]{1,0:T(8,128)(2,1)S(1)} %slice.42), channel_id=1, source_target_pairs={{0,16},{8,24},{16,32},{24,40},{32,48},{40,56},{48,0},{56,8},{64,80... | collective-permute-start | bytes 786440 | tf_op jit(solution)/shard_map/ppermute | solution.py:39
  88.2 4.8 %collective-permute-done.5.refs_4_ = bf16[512,256]{1,0:T(8,128)(2,1)S(1)} collective-permute-done((bf16[512,256]{1,0:T(8,128)(2,1)S(1)}, bf16[512,256]{1,0:T(8,128)(2,1)S(1)}, u32[]{:S(2)}, u32[]{:S(2)}) %collective-permute-start.5) | collective-permute-done | bytes 262176 | tf_op jit(solution)/shard_map/ppermute | solution.py:39
  93.0 2.7 %collective-permute-done.6.refs_5_ = bf16[512,256]{1,0:T(8,128)(2,1)S(1)} collective-permute-done((bf16[512,256]{1,0:T(8,128)(2,1)S(1)}, bf16[512,256]{1,0:T(8,128)(2,1)S(1)}, u32[]{:S(2)}, u32[]{:S(2)}) %collective-permute-start.6) | collective-permute-done | bytes 262176 | tf_op jit(solution)/shard_map/ppermute | solution.py:39
  95.7 1.6 collective-permute-start.8
  97.4 25.7 %shard_map.113 = (f32[2,4,512,128]{3,2,1,0:T(8,128)}, f32[2,4,512,128]{3,2,1,0:T(8,128)}) custom-call(s32[11]{0:T(128)S(1)} %concatenate.38.refs_0_, bf16[2,512,512]{2,1,0:T(8,128)(2,1)S(1)} %pad_maximum_fusion.2.refs_1_, bf16[1024,256]{1,0:T(8,128)(2,1)S(1)} %copy-done.5, bf16[1024,256]{1,0:T(8,128)(2,1)} %collective-permute-done.10.refs_3_, ...), custom_call_target="tpu_custom_call" | custom-call | flops 17179869184 | bytes 16777216 | tf_op jit(solution)/shard_map/pallas_call | solution.py:189
  123.1 2.5 %fusion.2 = (f32[1,4,512,128]{3,2,1,0:T(8,128)S(1)}, f32[1,4,512,128]{3,2,1,0:T(8,128)S(1)}, f32[1,4,512,128]{3,2,1,0:T(8,128)S(1)}, f32[1,4,512,128]{3,2,1,0:T(8,128)S(1)}) fusion(f32[2,4,512,128]{3,2,1,0:T(8,128)} %get-tuple-element.5, f32[2,4,512,128]{3,2,1,0:T(8,128)} %get-tuple-element.4), kind=kLoop, calls=%fused_computation.22 | loop fusion | bytes 8388608 | tf_op jit(solution)/shard_map/slice | solution.py:440
  125.7 1.2 copy-done.13
  126.8 5.8 %shard_map.115 = bf16[1,512,512]{2,1,0:T(8,128)(2,1)S(1)} custom-call(s32[10]{0:T(128)S(1)} %concatenate.40.refs_0_, bf16[1,512,512]{2,1,0:T(8,128)(2,1)} %bitcast.19.refs_1_, bf16[1536,256]{1,0:T(8,128)(2,1)S(1)} %collective-permute-done.2.refs_2_, bf16[1536,256]{1,0:T(8,128)(2,1)S(1)} %collective-permute-done.4.refs_3_, ...), custom_call_target="tpu_custom_call" | custom-call | flops 8589934592 | bytes 16777216 | tf_op jit(solution)/shard_map/pallas_call | solution.py:189
  132.7 22.8 %collective-permute-start.12 = (bf16[512,512]{1,0:T(8,128)(2,1)S(1)}, bf16[512,512]{1,0:T(8,128)(2,1)S(1)}, u32[]{:S(2)}, u32[]{:S(2)}) collective-permute-start(bf16[512,512]{1,0:T(8,128)(2,1)S(1)} %bitcast.32), channel_id=1, source_target_pairs={{0,120},{8,112},{16,104},{24,96},{32,88},{40,80},{48,72},{56,64},{... | collective-permute-start | bytes 1572872 | tf_op jit(solution)/shard_map/ppermute | solution.py:39
  155.5 23.9 %shard_map.114 = bf16[1,512,512]{2,1,0:T(8,128)(2,1)S(1)} custom-call(s32[10]{0:T(128)S(1)} %concatenate.32.refs_0_, bf16[1,512,512]{2,1,0:T(8,128)(2,1)S(1)} %get-tuple-element.12.refs_1_, bf16[1536,256]{1,0:T(8,128)(2,1)S(1)} %collective-permute-done.2.refs_2_, bf16[1536,256]{1,0:T(8,128)(2,1)S(1)} %collective-permute-done.4.refs_3_, ...), custom_call_target="tpu_custom_call" | custom-call | flops 8589934592 | bytes 16777216 | tf_op jit(solution)/shard_map/pallas_call | solution.py:189
  179.4 1.0 pad_maximum_fusion.3
  (71 shorter events, 10.1 us)
Async XLA Ops:
  0.6 10.9 %copy-start.8 = (bf16[2,8,512]{2,1,0:T(8,128)(2,1)S(1)}, bf16[2,8,512]{2,1,0:T(8,128)(2,1)}, u32[]{:S(2)}) copy-start(bf16[2,8,512]{2,1,0:T(8,128)(2,1)} %param.13) | copy-start | bytes 49156
  0.6 11.0 %copy-start.12 = (s32[128]{0:T(128)S(1)}, s32[128]{0:T(128)}, u32[]{:S(2)}) copy-start(s32[128]{0:T(128)} %param.19) | copy-start | bytes 1540
  0.7 42.8 %copy-start.9 = (s32[128,16]{0,1:T(8,128)S(1)}, s32[128,16]{0,1:T(8,128)}, u32[]{:S(2)}) copy-start(s32[128,16]{0,1:T(8,128)} %param.18) | copy-start | bytes 24580
  2.7 43.5 %copy-start.4 = (bf16[1024,256]{1,0:T(8,128)(2,1)}, bf16[1024,256]{1,0:T(8,128)(2,1)S(1)}, u32[]{:S(2)}) copy-start(bf16[1024,256]{1,0:T(8,128)(2,1)S(1)} %constant_dynamic-update-slice_fusion.refs_2_) | copy-start | bytes 1572868
  2.7 42.2 %collective-permute-start = (bf16[1024,256]{1,0:T(8,128)(2,1)S(1)}, bf16[1024,256]{1,0:T(8,128)(2,1)S(1)}, u32[]{:S(2)}, u32[]{:S(2)}) collective-permute-start(bf16[1024,256]{1,0:T(8,128)(2,1)S(1)} %constant_dynamic-update-slice_fusion.refs_2_), channel_id=1, source_target_pairs={{0,64},{8,72},{16,80},{24,88},{32,96},{40,104},{48,112},{56,120},{... | collective-permute-start | bytes 1572872 | tf_op jit(solution)/shard_map/ppermute | solution.py:39
  3.1 41.8 %collective-permute-start.1 = (bf16[1024,256]{1,0:T(8,128)(2,1)S(1)}, bf16[1024,256]{1,0:T(8,128)(2,1)S(1)}, u32[]{:S(2)}, u32[]{:S(2)}) collective-permute-start(bf16[1024,256]{1,0:T(8,128)(2,1)S(1)} %constant_dynamic-update-slice_fusion.refs_2_), channel_id=1, source_target_pairs={{0,16},{8,24},{16,32},{24,40},{32,48},{40,56},{48,0},{56,8},{64,80... | collective-permute-start | bytes 1572872 | tf_op jit(solution)/shard_map/ppermute | solution.py:39
  3.1 41.9 %collective-permute-start.3 = (bf16[1024,256]{1,0:T(8,128)(2,1)S(1)}, bf16[1024,256]{1,0:T(8,128)(2,1)S(1)}, u32[]{:S(2)}, u32[]{:S(2)}) collective-permute-start(bf16[1024,256]{1,0:T(8,128)(2,1)S(1)} %constant_dynamic-update-slice_fusion.refs_2_), channel_id=1, source_target_pairs={{0,48},{8,56},{16,0},{24,8},{32,16},{40,24},{48,32},{56,40},{64,11... | collective-permute-start | bytes 1572872 | tf_op jit(solution)/shard_map/ppermute | solution.py:39
  6.6 77.5 %collective-permute-start.9 = (bf16[512,512]{1,0:T(8,128)(2,1)}, bf16[512,512]{1,0:T(8,128)(2,1)}, u32[]{:S(2)}, u32[]{:S(2)}) collective-permute-start(bf16[512,512]{1,0:T(8,128)(2,1)} %get-tuple-element.13), channel_id=1, source_target_pairs={{0,120},{8,112},{16,104},{24,96},{32,88},{40,80},{48,72},{56,64},{... | collective-permute-start | bytes 1572872 | tf_op jit(solution)/shard_map/ppermute | solution.py:39
  44.9 6.4 %copy-start.6 = (bf16[128,128,128]{2,1,0:T(8,128)(2,1)S(1)}, bf16[128,128,128]{2,1,0:T(8,128)(2,1)}, u32[]{:S(2)}) copy-start(bf16[128,128,128]{2,1,0:T(8,128)(2,1)} %k_ref.1) | copy-start | bytes 12582916
  46.2 5.1 %copy-start.2 = (f32[128,8,128]{2,1,0:T(8,128)S(1)}, f32[128,8,128]{2,1,0:T(8,128)}, u32[]{:S(2)}) copy-start(f32[128,8,128]{2,1,0:T(8,128)} %convert_element_type.15.q_ref) | copy-start | bytes 1572868
  46.2 51.1 %collective-permute-start.11 = (bf16[3072,256]{1,0:T(8,128)(2,1)}, bf16[3072,256]{1,0:T(8,128)(2,1)}, u32[]{:S(2)}, u32[]{:S(2)}) collective-permute-start(bf16[3072,256]{1,0:T(8,128)(2,1)} %pad_maximum_fusion.1), channel_id=1, source_target_pairs={{0,8},{8,0},{16,24},{24,16},{32,40},{40,32},{48,56},{56,48},{64,72... | collective-permute-start | bytes 4718600 | tf_op jit(solution)/shard_map/ppermute | solution.py:39
  47.9 37.3 %collective-permute-start.2 = (bf16[1536,256]{1,0:T(8,128)(2,1)}, bf16[1536,256]{1,0:T(8,128)(2,1)S(1)}, u32[]{:S(2)}, u32[]{:S(2)}) collective-permute-start(bf16[1536,256]{1,0:T(8,128)(2,1)} %get-tuple-element.15), channel_id=1, source_target_pairs={{0,16},{8,24},{16,32},{24,40},{32,48},{40,56},{48,0},{56,8},{64,80... | collective-permute-start | bytes 2359304 | tf_op jit(solution)/shard_map/ppermute | solution.py:39
  51.3 35.9 %collective-permute-start.4 = (bf16[1536,256]{1,0:T(8,128)(2,1)}, bf16[1536,256]{1,0:T(8,128)(2,1)S(1)}, u32[]{:S(2)}, u32[]{:S(2)}) collective-permute-start(bf16[1536,256]{1,0:T(8,128)(2,1)} %get-tuple-element.14), channel_id=1, source_target_pairs={{0,48},{8,56},{16,0},{24,8},{32,16},{40,24},{48,32},{56,40},{64,11... | collective-permute-start | bytes 2359304 | tf_op jit(solution)/shard_map/ppermute | solution.py:39
  53.5 20.1 %copy-start.10 = (bf16[2,8,128]{2,1,0:T(8,128)(2,1)S(1)}, bf16[2,8,128]{2,1,0:T(8,128)(2,1)}, u32[]{:S(2)}) copy-start(bf16[2,8,128]{2,1,0:T(8,128)(2,1)} %param.14) | copy-start | bytes 12292
  53.5 20.7 %copy-start.11 = (bf16[2,8,128]{2,1,0:T(8,128)(2,1)S(1)}, bf16[2,8,128]{2,1,0:T(8,128)(2,1)}, u32[]{:S(2)}) copy-start(bf16[2,8,128]{2,1,0:T(8,128)(2,1)} %param.15) | copy-start | bytes 12292
  62.3 18.0 %all-to-all-start = ((bf16[128,16,128]{2,1,0:T(8,128)(2,1)}), bf16[128,16,128]{2,1,0:T(8,128)(2,1)}, u32[]{:S(2)}, u32[]{:S(2)}) async-start(bf16[128,16,128]{2,1,0:T(8,128)(2,1)} %copy-done.3), calls=%async_computation | async-start | bytes 1048576 | tf_op jit(solution)/shard_map/all_to_all | solution.py:455
  72.5 24.9 %collective-permute-start.10 = (bf16[1024,256]{1,0:T(8,128)(2,1)}, bf16[1024,256]{1,0:T(8,128)(2,1)}, u32[]{:S(2)}, u32[]{:S(2)}) collective-permute-start(bf16[1024,256]{1,0:T(8,128)(2,1)} %copy-done.4), channel_id=1, source_target_pairs={{0,8},{8,0},{16,24},{24,16},{32,40},{40,32},{48,56},{56,48},{64,72... | collective-permute-start | bytes 1572872 | tf_op jit(solution)/shard_map/ppermute | solution.py:39
  85.3 7.7 %collective-permute-start.5 = (bf16[512,256]{1,0:T(8,128)(2,1)S(1)}, bf16[512,256]{1,0:T(8,128)(2,1)S(1)}, u32[]{:S(2)}, u32[]{:S(2)}) collective-permute-start(bf16[512,256]{1,0:T(8,128)(2,1)S(1)} %slice.42), channel_id=1, source_target_pairs={{0,16},{8,24},{16,32},{24,40},{32,48},{40,56},{48,0},{56,8},{64,80... | collective-permute-start | bytes 786440 | tf_op jit(solution)/shard_map/ppermute | solution.py:39
  87.2 10.1 %copy-start.1 = (bf16[1024,256]{1,0:T(8,128)(2,1)S(1)}, bf16[1024,256]{1,0:T(8,128)(2,1)}, u32[]{:S(2)}) copy-start(bf16[1024,256]{1,0:T(8,128)(2,1)} %copy-done) | copy-start | bytes 1572868
  87.2 10.1 %copy-start.5 = (bf16[1024,256]{1,0:T(8,128)(2,1)S(1)}, bf16[1024,256]{1,0:T(8,128)(2,1)}, u32[]{:S(2)}) copy-start(bf16[1024,256]{1,0:T(8,128)(2,1)} %copy-done.4) | copy-start | bytes 1572868
  87.2 8.4 %collective-permute-start.6 = (bf16[512,256]{1,0:T(8,128)(2,1)S(1)}, bf16[512,256]{1,0:T(8,128)(2,1)S(1)}, u32[]{:S(2)}, u32[]{:S(2)}) collective-permute-start(bf16[512,256]{1,0:T(8,128)(2,1)S(1)} %slice.43), channel_id=1, source_target_pairs={{0,48},{8,56},{16,0},{24,8},{32,16},{40,24},{48,32},{56,40},{64,11... | collective-permute-start | bytes 786440 | tf_op jit(solution)/shard_map/ppermute | solution.py:39
  87.4 38.2 %collective-permute-start.7 = (bf16[3072,256]{1,0:T(8,128)(2,1)S(1)}, bf16[3072,256]{1,0:T(8,128)(2,1)S(1)}, u32[]{:S(2)}, u32[]{:S(2)}) collective-permute-start(bf16[3072,256]{1,0:T(8,128)(2,1)S(1)} %pad_maximum_fusion), channel_id=1, source_target_pairs={{0,8},{8,0},{16,24},{24,16},{32,40},{40,32},{48,56},{56,48},{64,72... | collective-permute-start | bytes 4718600 | tf_op jit(solution)/shard_map/ppermute | solution.py:39
  95.7 29.9 %collective-permute-start.8 = (bf16[1024,256]{1,0:T(8,128)(2,1)S(1)}, bf16[1024,256]{1,0:T(8,128)(2,1)S(1)}, u32[]{:S(2)}, u32[]{:S(2)}) collective-permute-start(bf16[1024,256]{1,0:T(8,128)(2,1)S(1)} %pad_maximum_fusion.6), channel_id=1, source_target_pairs={{0,8},{8,0},{16,24},{24,16},{32,40},{40,32},{48,56},{56,48},{64,72... | collective-permute-start | bytes 1572872 | tf_op jit(solution)/shard_map/ppermute | solution.py:39
  132.7 46.7 %collective-permute-start.12 = (bf16[512,512]{1,0:T(8,128)(2,1)S(1)}, bf16[512,512]{1,0:T(8,128)(2,1)S(1)}, u32[]{:S(2)}, u32[]{:S(2)}) collective-permute-start(bf16[512,512]{1,0:T(8,128)(2,1)S(1)} %bitcast.32), channel_id=1, source_target_pairs={{0,120},{8,112},{16,104},{24,96},{32,88},{40,80},{48,72},{56,64},{... | collective-permute-start | bytes 1572872 | tf_op jit(solution)/shard_map/ppermute | solution.py:39
  (4 other events, 5.9 us)

commit v2 on v1

--- a/solution.py
+++ b/solution.py
@@ -19,6 +19,7 @@
 VMEM = pl.BlockSpec(memory_space=pltpu.VMEM)
 SMEM = pl.BlockSpec(memory_space=pltpu.SMEM)
 ANY = pl.BlockSpec(memory_space=pl.ANY)
+TINY = pl.CostEstimate(flops=1, bytes_accessed=1, transcendentals=0)
 NT = (((1,), (1,)), ((), ()))
 
 
@@ -39,13 +40,19 @@
     return lax.ppermute(value, "inst", pairs)
 
 
-def flash_kernel(half_count, sources, has_state, final, diag, *refs):
+def after(values, earlier):
+    return lax.optimization_barrier((*values, *earlier))[: len(values)]
+
+
+def flash_kernel(half_count, sources, has_state, final, diag, diag_slot, *refs):
     refs = list(refs)
-    meta, q_ref = refs.pop(0), refs.pop(0)
+    meta = refs.pop(0)
+    first_id = SLOTS if has_state else 0
+    q_refs = [refs.pop(0) for _ in range(half_count)]
     kv_refs = [refs.pop(0) for _ in range(1 + max(src for src, *_ in sources))]
     state_in = [refs.pop(0) for _ in range(2)] if has_state else None
-    outs = [refs.pop(0) for _ in range(1 if final else 2)]
-    kv, qs, acc, top, scores, row_top, items, sem = refs
+    outs = [refs.pop(0) for _ in range(half_count if final else 2)]
+    kv, qs, acc, top, scores, row_top, items, sem, *old = refs
 
     copies = [
         pltpu.make_async_copy(
@@ -57,30 +64,28 @@
     ]
     for copy in copies:
         copy.start()
+    state_copies = []
+    if has_state:
+        state_copies = [
+            pltpu.make_async_copy(state_in[k], old[k], sem.at[len(sources) + k]) for k in range(2)
+        ]
+    for copy in state_copies:
+        copy.start()
 
     for half in range(half_count):
         for h in range(HEADS):
-            scaled = q_ref[half, :, h * HD : (h + 1) * HD].astype(jnp.float32) * SCALE2
+            scaled = q_refs[half][:ROWS, h * HD : (h + 1) * HD].astype(jnp.float32) * SCALE2
             high = scaled.astype(jnp.bfloat16)
             qs[half, h, :, :HD] = high
             qs[half, h, :, HD:] = (scaled - high.astype(jnp.float32)).astype(jnp.bfloat16)
-    if has_state:
-        lane = lax.broadcasted_iota(jnp.int32, (ROWS, HD), 1)
-        for half in range(half_count):
-            for h in range(HEADS):
-                acc[half, h, :, :HD] = state_in[0][half, h]
-                stat = state_in[1][half, h]
-                top[half, h] = jnp.broadcast_to(stat[:, :1], (ROWS, HD))
-                acc[half, h, :, HD:] = jnp.broadcast_to(stat[:, HD - 1 :], (ROWS, HD))
-    else:
-        acc[...] = jnp.zeros_like(acc)
-        top[...] = jnp.full_like(top, LOW)
+    acc[...] = jnp.zeros_like(acc)
+    top[...] = jnp.full_like(top, LOW)
 
     count = jnp.int32(0)
     for half in range(half_count):
-        limit = meta[SLOTS + half]
+        limit = meta[2 * SLOTS + half]
         for slot in range(SLOTS):
-            wanted = meta[slot] < limit
+            wanted = meta[first_id + slot] < limit
 
             @pl.when(wanted)
             def _(count=count, half=half, slot=slot):
@@ -88,7 +93,7 @@
 
             count = count + wanted.astype(jnp.int32)
 
-    for copy in copies:
+    for copy in copies if diag_slot is None else copies[:1]:
         copy.wait()
 
     ones = jnp.ones((KEYS, HD), jnp.bfloat16)
@@ -112,7 +117,7 @@
 
     if diag is not None:
         half, first_row = diag
-        slot = meta[SLOTS + half_count]
+        slot = meta[2 * SLOTS + half_count] if diag_slot is None else diag_slot
         for r in range(ROWS // CHUNK):
             seen = first_row + (r + 1) * CHUNK
             key_rows = kv[slot, :seen, :HD]
@@ -131,6 +136,9 @@
                     half, h, r * CHUNK, s, jnp.max(s, axis=-1, keepdims=True), kv[slot, :seen, HD:]
                 )
 
+    for copy in [] if diag_slot is None else copies[1:]:
+        copy.wait()
+
     def place(item):
         code = items[item]
         return code // SLOTS, code % SLOTS
@@ -165,29 +173,41 @@
             produce(jnp.minimum(item + 1, count - 1), 0)
             consume(item, 1)
 
+    for copy in state_copies:
+        copy.wait()
     for half in range(half_count):
         for h in range(HEADS):
+            if has_state:
+                old_top, old_sum = old[1][half, h, :, :1], old[1][half, h, :, HD - 1 :]
+                new_top = jnp.maximum(old_top, top[half, h])
+                old_factor = jnp.exp2(old_top - new_top)
+                factor = jnp.exp2(top[half, h] - new_top)
+                value = acc[half, h, :, :HD] * factor + old[0][half, h] * old_factor
+                weight = acc[half, h, :, HD:] * factor + old_sum * old_factor
+            else:
+                value, weight = acc[half, h, :, :HD], acc[half, h, :, HD:]
             if final:
-                outs[0][half, :, h * HD : (h + 1) * HD] = (
-                    acc[half, h, :, :HD] / acc[half, h, :, HD:]
-                ).astype(jnp.bfloat16)
+                outs[half][:ROWS, h * HD : (h + 1) * HD] = (value / weight).astype(jnp.bfloat16)
             else:
                 lane = lax.broadcasted_iota(jnp.int32, (ROWS, HD), 1)
-                outs[0][half, h] = acc[half, h, :, :HD]
-                outs[1][half, h] = jnp.where(lane < HD // 2, top[half, h], acc[half, h, :, HD:])
-
-
-def flash(meta, queries, kv_arrays, sources, state=None, final=False, diag=None):
-    half_count = queries.shape[0]
+                outs[0][half, h] = value
+                outs[1][half, h] = jnp.where(lane < HD // 2, top[half, h], weight)
+
+
+def flash(meta, queries, kv_arrays, sources, state=None, final=False, diag=None, diag_slot=None):
+    half_count = len(queries)
     if final:
-        out_shape = [jax.ShapeDtypeStruct((half_count, ROWS, HEADS * HD), jnp.bfloat16)]
+        out_shape = [
+            jax.ShapeDtypeStruct((rows, HEADS * HD), jnp.bfloat16) for rows in (2 * ROWS, ROWS)
+        ]
     else:
         out_shape = [jax.ShapeDtypeStruct((half_count, HEADS, ROWS, HD), jnp.float32)] * 2
-    operands = [meta, queries, *kv_arrays, *(state or [])]
-    in_specs = [SMEM, VMEM] + [ANY] * len(kv_arrays) + [VMEM] * (2 if state else 0)
-    work = half_count * SLOTS * HEADS * ROWS * KEYS // 2
+    operands = [meta, *queries, *kv_arrays, *(state or [])]
+    in_specs = [SMEM] + [VMEM] * half_count + [ANY] * (len(kv_arrays) + (2 if state else 0))
     return pl.pallas_call(
-        functools.partial(flash_kernel, half_count, sources, state is not None, final, diag),
+        functools.partial(
+            flash_kernel, half_count, sources, state is not None, final, diag, diag_slot
+        ),
         out_shape=out_shape,
         in_specs=in_specs,
         out_specs=[VMEM] * len(out_shape),
@@ -199,12 +219,11 @@
             pltpu.VMEM((2, HEADS, CHUNK, KEYS), jnp.float32),
             pltpu.VMEM((2, HEADS, CHUNK, HD), jnp.float32),
             pltpu.SMEM((2 * SLOTS,), jnp.int32),
-            pltpu.SemaphoreType.DMA((len(sources),)),
+            pltpu.SemaphoreType.DMA((len(sources) + 2,)),
+            *[pltpu.VMEM(part.shape, jnp.float32) for part in state or []],
         ],
-        compiler_params=pltpu.CompilerParams(vmem_limit_bytes=48 << 20),
-        cost_estimate=pl.CostEstimate(
-            flops=work * HD * 4 * 2, bytes_accessed=16 << 20, transcendentals=work
-        ),
+        compiler_params=pltpu.CompilerParams(vmem_limit_bytes=58 << 20),
+        cost_estimate=TINY,
     )(*operands)
 
 
@@ -227,8 +246,8 @@
     for b in range(0, GROUP, 2):
         pair = jnp.concatenate(
             [
-                jnp.concatenate([q_ref[reqs[b]], zero], axis=1),
-                jnp.concatenate([zero, q_ref[reqs[b + 1]]], axis=1),
+                jnp.concatenate([q_ref[reqs[b]].astype(jnp.float32), zero], axis=1),
+                jnp.concatenate([zero, q_ref[reqs[b + 1]].astype(jnp.float32)], axis=1),
             ],
             axis=0,
         )
@@ -293,18 +312,17 @@
             scratch_shapes=[pltpu.VMEM((GROUP * QROWS, GROUP * HD), jnp.bfloat16), state, state, state],
         ),
         compiler_params=pltpu.CompilerParams(
-            dimension_semantics=("arbitrary",), vmem_limit_bytes=32 << 20
+            dimension_semantics=("arbitrary",), vmem_limit_bytes=58 << 20
         ),
-        cost_estimate=pl.CostEstimate(
-            flops=1 << 32, bytes_accessed=9 << 20, transcendentals=1 << 20
-        ),
+        cost_estimate=TINY,
     )(owner, live, queries, k_cache, v_cache)
 
 
 def merge_kernel(parts_ref, q_ref, k_ref, v_ref, out_ref):
     source_count, req_count = parts_ref.shape[0], parts_ref.shape[1]
+    k_new, v_new = k_ref[...].astype(jnp.float32), v_ref[...].astype(jnp.float32)
     for r in range(req_count):
-        queries = q_ref[r]
+        queries = q_ref[r].astype(jnp.float32)
         row = lax.broadcasted_iota(jnp.int32, (QROWS, 1), 0)
         levels, pieces = [], []
         for s in range(source_count):
@@ -313,25 +331,26 @@
             levels.append(terms[:, 0:1] + terms[:, 1:2] + terms[:, 2:3])
             pieces.append(both[:QROWS])
         for n in range(2):
-            key = k_ref[n, r : r + 1, :]
+            key = k_new[n, r : r + 1, :]
             score = jnp.sum(queries * key, axis=-1, keepdims=True) * SCALE2
             if n:
                 score = jnp.where(row >= n * HEADS, score, LOW)
             levels.append(score)
-            pieces.append(jnp.broadcast_to(v_ref[n, r : r + 1, :], (QROWS, HD)))
+            pieces.append(jnp.broadcast_to(v_new[n, r : r + 1, :], (QROWS, HD)))
         highest = functools.reduce(jnp.maximum, levels)
         shares = [jnp.exp2(level - highest) for level in levels]
         result = functools.reduce(jnp.add, [w * p for w, p in zip(shares, pieces)])
-        out_ref[r] = result / functools.reduce(jnp.add, shares)
+        out_ref[r] = (result / functools.reduce(jnp.add, shares)).astype(jnp.bfloat16)
 
 
 def decode_merge(parts, queries, k_new, v_new):
     return pl.pallas_call(
         merge_kernel,
-        out_shape=jax.ShapeDtypeStruct(queries.shape, jnp.float32),
+        out_shape=jax.ShapeDtypeStruct(queries.shape, jnp.bfloat16),
         in_specs=[VMEM] * 4,
         out_specs=VMEM,
-    )(parts, queries, k_new.astype(jnp.float32), v_new.astype(jnp.float32))
+        cost_estimate=TINY,
+    )(parts, queries, k_new, v_new)
 
 
 def body(
@@ -352,22 +371,42 @@
 
     own_queries = q_decode.reshape(steps, req_local, HEADS, HD).transpose(1, 0, 2, 3)
     own_queries = own_queries.reshape(req_local, QROWS, HD)
-    every_query = lax.all_gather(own_queries, "inst", axis=0, tiled=True)
+    copies = jnp.broadcast_to(own_queries, (16, req_local, QROWS, HD)).reshape(-1, QROWS, HD)
+    every_query = lax.all_to_all(copies, "inst", 0, 0, tiled=True)
 
     own = jnp.concatenate([k_prefill, v_prefill], axis=1)
     up = permute(own, moves(0, 1, 0))
     down = permute(own, moves(0, -1, 0))
     across = permute(own, moves(1, 0, 0))
     beside = permute(own, moves(0, 0, 1))
+    up, down, across = after([up, down, across], [every_query])
     mirror = [(i, 15 - i) for i in range(16)]
-    other_rows = permute(q_prefill[ROWS:], mirror)
-    queries = jnp.stack([q_prefill[:ROWS], other_rows])
-
     up_more = permute(jnp.concatenate([across, up[:ROWS]]), moves(0, 1, 0))
     down_more = permute(jnp.concatenate([across, down[ROWS:]]), moves(0, -1, 0))
     beside_near = permute(jnp.concatenate([up, down, across]), moves(0, 0, 1))
-
-    limits = jnp.stack([me, 15 - me])
+    block_count, block_len = k_cache.shape[:2]
+    width = block_table.shape[1]
+    global_id = me * block_count + jnp.arange(block_count, dtype=jnp.int32)
+    matches = block_table.reshape(-1)[None, :] == global_id[:, None]
+    place = jnp.arange(block_table.size, dtype=jnp.int32)[None, :]
+    flat = jnp.sum(jnp.where(matches, place, 0), axis=1)
+    owner = flat // width
+    left = req_lengths[:, None] - jnp.arange(width, dtype=jnp.int32)[None, :] * block_len
+    left = jnp.clip(left, 0, block_len).reshape(-1)
+    live = jnp.sum(jnp.where(matches, left[None, :], 0), axis=1)
+    every_query = after([every_query], [beside_near])[0]
+    parts = decode_cache(owner, live, every_query, k_cache, v_cache)
+    received = lax.all_to_all(parts, "inst", 0, 0, tiled=True)
+
+    second_rows = after([q_prefill], [parts])[0][ROWS:]
+    other_rows = permute(second_rows, mirror)
+    queries = [q_prefill, other_rows]
+
+    up_more, down_more = after([up_more, down_more], [second_rows])
+    up_last = permute(up_more[:KEYS], moves(0, 1, 0))
+    down_last = permute(down_more[:KEYS], moves(0, -1, 1))
+    beside_far = permute(jnp.concatenate([up_more, down_more]), moves(0, 0, 1))
+
     near_ids = [
         me,
         index_of(z, y, c + 1),
@@ -378,21 +417,6 @@
         index_of(z, y + 1, c + 1),
         index_of(z + 1, y, c + 1),
     ]
-    near_meta = jnp.concatenate([jnp.stack(near_ids), limits, jnp.zeros((1,), jnp.int32)])
-    near_sources = [(k, 0, KEYS, k, 0) for k in range(5)]
-    near_sources += [(5, k * KEYS, KEYS, 5 + k, 0) for k in range(3)]
-    state = flash(
-        near_meta.astype(jnp.int32),
-        queries,
-        [own, beside, up, down, across, beside_near],
-        near_sources,
-        diag=(0, 0),
-    )
-
-    up_last = permute(up_more[:ROWS], moves(0, 1, 0))
-    down_last = permute(down_more[ROWS:KEYS], moves(0, -1, 0))
-    beside_far = permute(jnp.concatenate([up_more, down_more]), moves(0, 0, 1))
-    beside_last = permute(jnp.concatenate([up_last, down_last]), moves(0, 0, 1))
     far_ids = [
         index_of(z, y + 2, c),
         index_of(z + 1, y + 3, c),
@@ -403,63 +427,49 @@
         index_of(z + 1, y + 1, c + 1),
         index_of(z + 1, y + 2, c + 1),
     ]
-    far_arrays = [up_more, down_more, up_last, down_last, beside_far, beside_last]
+    near_sources = [(k, 0, KEYS, k, 0) for k in range(5)]
+    near_sources += [(5, k * KEYS, KEYS, 5 + k, 0) for k in range(3)]
+    mirror_slot = jnp.where(y % 2 == 0, 5, 6)
+    numbers = jnp.stack([*near_ids, *far_ids, me, 15 - me, mirror_slot]).astype(jnp.int32)
+    own = after([own], [parts])[0]
+    state = flash(
+        numbers,
+        queries,
+        [own, beside, up, down, across, beside_near],
+        near_sources,
+        diag=(0, 0),
+        diag_slot=0,
+    )
+
     both = KEYS + ROWS
     far_sources = [
         (0, KEYS, ROWS, 0, 0),
         (1, KEYS, ROWS, 0, ROWS),
         (0, 0, KEYS, 1, 0),
         (1, 0, KEYS, 2, 0),
-        (2, 0, ROWS, 3, 0),
-        (3, 0, ROWS, 3, ROWS),
+        (2, 0, KEYS, 3, 0),
         (4, KEYS, ROWS, 4, 0),
         (4, both + KEYS, ROWS, 4, ROWS),
         (4, 0, KEYS, 5, 0),
         (4, both, KEYS, 6, 0),
-        (5, 0, KEYS, 7, 0),
+        (3, 0, KEYS, 7, 0),
     ]
-    mirror_slot = jnp.where(y % 2 == 0, 5, 6)
-    far_ids = jnp.stack(far_ids)
-    other_meta = jnp.concatenate([far_ids, limits[1:], mirror_slot[None]]).astype(jnp.int32)
-    own_meta = jnp.concatenate([far_ids, limits[:1], mirror_slot[None]]).astype(jnp.int32)
-    (other_out,) = flash(
-        other_meta,
-        queries[1:],
-        far_arrays,
+    *state, received = lax.optimization_barrier((*state, received))
+    received = received.reshape(-1, req_local, 2 * QROWS, HD)
+    decode_out = decode_merge(received, own_queries, k_new, v_new)
+    decode_out = decode_out.reshape(req_local, steps, HEADS * HD).transpose(1, 0, 2)
+
+    own_out, other_out = flash(
+        numbers,
+        queries,
+        [up_more, down_more, up_last, down_last, beside_far],
         far_sources,
-        state=[part[1:] for part in state],
+        state=state,
         final=True,
-        diag=(0, ROWS),
+        diag=(1, ROWS),
     )
-    last_rows = permute(other_out[0], mirror)
-    (own_out,) = flash(
-        own_meta,
-        queries[:1],
-        far_arrays,
-        far_sources,
-        state=[part[:1] for part in state],
-        final=True,
-    )
-
-    block_count, block_len = k_cache.shape[:2]
-    width = block_table.shape[1]
-    global_id = me * block_count + jnp.arange(block_count, dtype=jnp.int32)
-    matches = block_table.reshape(-1)[None, :] == global_id[:, None]
-    place = jnp.arange(block_table.size, dtype=jnp.int32)[None, :]
-    flat = jnp.sum(jnp.where(matches, place, 0), axis=1)
-    owner = flat // width
-    left = req_lengths[:, None] - jnp.arange(width, dtype=jnp.int32)[None, :] * block_len
-    left = jnp.clip(left, 0, block_len).reshape(-1)
-    live = jnp.sum(jnp.where(matches, left[None, :], 0), axis=1)
-    parts = decode_cache(owner, live, every_query.astype(jnp.float32), k_cache, v_cache)
-    parts = lax.all_to_all(parts, "inst", 0, 0, tiled=True)
-    parts = parts.reshape(-1, req_local, 2 * QROWS, HD)
-    result = decode_merge(parts, own_queries.astype(jnp.float32), k_new, v_new)
-    result = result.astype(jnp.bfloat16).reshape(req_local, steps, HEADS * HD)
-    decode_out = result.transpose(1, 0, 2)
-
-    prefill_out = jnp.concatenate([own_out[0], last_rows])
-    return prefill_out, decode_out
+    last_rows = permute(other_out, mirror)
+    return lax.dynamic_update_slice(own_out, last_rows, (ROWS, 0)), decode_out
 
 
 def solution(mesh):

time: 181 us -> 146 us (0.81)
  the two profiles are of different devices: /device:TPU:127 before, /device:TPU:1 now
where the time goes in v2:
time: 146 us
  Pallas kernels  69.7 us (48%)
  starting transfers between devices  28.8 us (20%)
  waiting for transfers between devices  15.6 us (11%)
  blocking collectives  14.6 us (10%)
  local copies, waits for them, and re-layouts  10.5 us (7%)
  other arithmetic  5.57 us (4%)
    pallas_call x2, Pallas kernels, flash(): pl.pallas_call(functools.partial(flash_kernel, half_count, sources, state...  55.9 us
    ppermute x12, starting transfers between devices, permute(): return lax.ppermute(value, 'inst', pairs)  25.2 us
    ppermute x12, waiting for transfers between devices, permute(): return lax.ppermute(value, 'inst', pairs)  15.6 us
    all_to_all x1, blocking collectives, body(): every_query = lax.all_to_all(copies, 'inst', 0, 0, tiled=True)  14.6 us
    pallas_call x1, Pallas kernels, decode_cache(): pl.pallas_call(decode_kernel, out_shape=jax.ShapeDtypeStruct((req_count,...  11.5 us
    all_to_all x1, starting transfers between devices, body(): received = lax.all_to_all(parts, 'inst', 0, 0, tiled=True)  3.59 us
    unnamed x32, local copies, waits for them, and re-layouts  3.1 us
  transfers between devices with their start and end apart: 13, of which 3 were waited for; matrix products, arithmetic and copies ran while one was open for 6% of the time, Pallas kernels for 31%

profile of v2, /device:TPU:1, one launch (start us, length us, event | category | flops | bytes accessed | tf_op | source)
XLA Modules:
  0.0 145.7 jit_solution(7298326469955448467)
XLA Ops:
  0.6 1.0 constant_dynamic-update-slice_fusion.1
  1.6 1.0 constant_dynamic-update-slice_fusion.refs_3_
  2.7 2.2 %collective-permute-start = (bf16[1024,256]{1,0:T(8,128)(2,1)S(1)}, bf16[1024,256]{1,0:T(8,128)(2,1)S(1)}, u32[]{:S(2)}, u32[]{:S(2)}) collective-permute-start(bf16[1024,256]{1,0:T(8,128)(2,1)S(1)} %constant_dynamic-update-slice_fusion.refs_3_), channel_id=1, source_target_pairs={{0,16},{8,24},{16,32},{24,40},{32,48},{40,56},{48,0},{56,8},{64,80... | collective-permute-start | bytes 1572872 | tf_op jit(solution)/shard_map/ppermute | solution.py:40
  4.9 1.5 %collective-permute-start.1 = (bf16[1024,256]{1,0:T(8,128)(2,1)S(1)}, bf16[1024,256]{1,0:T(8,128)(2,1)S(1)}, u32[]{:S(2)}, u32[]{:S(2)}) collective-permute-start(bf16[1024,256]{1,0:T(8,128)(2,1)S(1)} %constant_dynamic-update-slice_fusion.refs_3_), channel_id=1, source_target_pairs={{0,48},{8,56},{16,0},{24,8},{32,16},{40,24},{48,32},{56,40},{64,11... | collective-permute-start | bytes 1572872 | tf_op jit(solution)/shard_map/ppermute | solution.py:40
  6.4 3.6 %collective-permute-start.2 = (bf16[1024,256]{1,0:T(8,128)(2,1)S(1)}, bf16[1024,256]{1,0:T(8,128)(2,1)S(1)}, u32[]{:S(2)}, u32[]{:S(2)}) collective-permute-start(bf16[1024,256]{1,0:T(8,128)(2,1)S(1)} %constant_dynamic-update-slice_fusion.refs_3_), channel_id=1, source_target_pairs={{0,64},{8,72},{16,80},{24,88},{32,96},{40,104},{48,112},{56,120},{... | collective-permute-start | bytes 1572872 | tf_op jit(solution)/shard_map/ppermute | solution.py:40
  10.7 14.6 %all_to_all.10.q_ref = bf16[128,8,128]{2,1,0:T(8,128)(2,1)} all-to-all(bf16[128,8,128]{2,1,0:T(8,128)(2,1)S(1)} %bitcast.28), channel_id=1, replica_groups=mesh['inst'=16,'tp'=8] {'inst'}, dimensions={0} | all-to-all | bytes 524288 | tf_op jit(solution)/shard_map/all_to_all | solution.py:375
  25.4 1.4 pad_maximum_fusion
  27.1 1.3 pad_maximum_fusion.2
  28.4 0.9 collective-permute-start.5
  29.2 1.8 %collective-permute-start.6 = (bf16[1536,256]{1,0:T(8,128)(2,1)}, bf16[1536,256]{1,0:T(8,128)(2,1)S(1)}, u32[]{:S(2)}, u32[]{:S(2)}) collective-permute-start(bf16[1536,256]{1,0:T(8,128)(2,1)} %get-tuple-element.34), channel_id=1, source_target_pairs={{0,48},{8,56},{16,0},{24,8},{32,16},{40,24},{48,32},{56,40},{64,11... | collective-permute-start | bytes 2359304 | tf_op jit(solution)/shard_map/ppermute | solution.py:40
  31.4 0.9 fusion.1
  32.8 11.5 %shard_map.113 = bf16[128,16,128]{2,1,0:T(8,128)(2,1)} custom-call(s32[128]{0:T(128)} %and_select_fusion.owner, s32[128]{0:T(128)} %get-tuple-element.32.live, bf16[128,8,128]{2,1,0:T(8,128)(2,1)} %all_to_all.10.q_ref, bf16[128,128,128]{2,1,0:T(8,128)(2,1)} %k_ref.2, bf16[128,128,128]{2,1,0:T(8,128)(2,1)} %v_ref.2), custom_call_target="tpu_custom_call" | custom-call | flops 1 | bytes 1 | tf_op jit(solution)/shard_map/pallas_call | solution.py:300
  45.2 3.4 %collective-permute-done.5.refs_3_ = bf16[1536,256]{1,0:T(8,128)(2,1)S(1)} collective-permute-done((bf16[1536,256]{1,0:T(8,128)(2,1)}, bf16[1536,256]{1,0:T(8,128)(2,1)S(1)}, u32[]{:S(2)}, u32[]{:S(2)}) %collective-permute-start.5) | collective-permute-done | bytes 786464 | tf_op jit(solution)/shard_map/ppermute | solution.py:40
  48.6 1.4 pad_maximum_fusion.1
  50.0 1.1 collective-permute-start.9
  51.2 5.8 %collective-permute-start.4 = (bf16[512,512]{1,0:T(8,128)(2,1)}, bf16[512,512]{1,0:T(8,128)(2,1)S(1)}, u32[]{:S(2)}, u32[]{:S(2)}) collective-permute-start(bf16[512,512]{1,0:T(8,128)(2,1)} %slice.15), channel_id=1, source_target_pairs={{0,120},{8,112},{16,104},{24,96},{32,88},{40,80},{48,72},{56,64},{... | collective-permute-start | bytes 1572872 | tf_op jit(solution)/shard_map/ppermute | solution.py:40
  58.6 2.8 %collective-permute-start.8 = (bf16[1024,256]{1,0:T(8,128)(2,1)}, bf16[1024,256]{1,0:T(8,128)(2,1)S(1)}, u32[]{:S(2)}, u32[]{:S(2)}) collective-permute-start(bf16[1024,256]{1,0:T(8,128)(2,1)} %slice.19), channel_id=1, source_target_pairs={{0,56},{8,48},{16,8},{24,0},{32,24},{40,16},{48,40},{56,32},{64,12... | collective-permute-start | bytes 1572872 | tf_op jit(solution)/shard_map/ppermute | solution.py:40
  61.5 3.6 %all-to-all-start.1 = ((bf16[128,16,128]{2,1,0:T(8,128)(2,1)}), bf16[128,16,128]{2,1,0:T(8,128)(2,1)S(1)}, u32[]{:S(2)}, u32[]{:S(2)}) async-start(bf16[128,16,128]{2,1,0:T(8,128)(2,1)} %shard_map.113), calls=%async_computation.1 | async-start | bytes 1048576 | tf_op jit(solution)/shard_map/all_to_all | solution.py:399
  65.9 3.7 %collective-permute-done.4.refs_2_ = bf16[512,512]{1,0:T(8,128)(2,1)S(1)} collective-permute-done((bf16[512,512]{1,0:T(8,128)(2,1)}, bf16[512,512]{1,0:T(8,128)(2,1)S(1)}, u32[]{:S(2)}, u32[]{:S(2)}) %collective-permute-start.4) | collective-permute-done | bytes 524320 | tf_op jit(solution)/shard_map/ppermute | solution.py:40
  70.4 31.1 %shard_map.114 = (f32[2,4,512,128]{3,2,1,0:T(8,128)}, f32[2,4,512,128]{3,2,1,0:T(8,128)}) custom-call(s32[19]{0:T(128)} %stack.76.refs_0_, bf16[1024,512]{1,0:T(8,128)(2,1)} %refs_1_.3, bf16[512,512]{1,0:T(8,128)(2,1)} %copy-done.6, bf16[1024,256]{1,0:T(8,128)(2,1)} %copy-done.8, bf16[1024,256]{1,0:T(8,128)(2,1)} %collective-permute-done.10.refs_4_, ...), custom_call_target="tpu_custom_call" | custom-call | flops 1 | bytes 1 | tf_op jit(solution)/shard_map/pallas_call | solution.py:207
  102.6 24.8 %shard_map.115 = (bf16[1024,512]{1,0:T(8,128)(2,1)}, bf16[512,512]{1,0:T(8,128)(2,1)}) custom-call(s32[19]{0:T(128)} %stack.76.refs_0_, bf16[1024,512]{1,0:T(8,128)(2,1)} %refs_1_.3, bf16[512,512]{1,0:T(8,128)(2,1)} %copy-done.6, bf16[1536,256]{1,0:T(8,128)(2,1)} %copy-done.1, bf16[1536,256]{1,0:T(8,128)(2,1)} %copy-done.2, bf16[1024,256]{1,0:T(8,128)(2,1)} %copy-done.10, ...), custom_call_target="tpu_custom_call" | custom-call | flops 1 | bytes 1 | tf_op jit(solution)/shard_map/pallas_call | solution.py:207
  127.4 5.4 %collective-permute-start.11 = (bf16[512,512]{1,0:T(8,128)(2,1)}, bf16[512,512]{1,0:T(8,128)(2,1)S(1)}, u32[]{:S(2)}, u32[]{:S(2)}) collective-permute-start(bf16[512,512]{1,0:T(8,128)(2,1)} %get-tuple-element.30), channel_id=1, source_target_pairs={{0,120},{8,112},{16,104},{24,96},{32,88},{40,80},{48,72},{56,64},{... | collective-permute-start | bytes 1572872 | tf_op jit(solution)/shard_map/ppermute | solution.py:40
  132.8 2.3 %shard_map.116 = bf16[8,8,128]{2,1,0:T(8,128)(2,1)} custom-call(bf16[16,8,16,128]{3,2,1,0:T(8,128)(2,1)} %bitcast.27, bf16[8,8,128]{2,1,0:T(8,128)(2,1)} %bitcast.30, bf16[2,8,128]{2,1,0:T(8,128)(2,1)} %k_ref.3, bf16[2,8,128]{2,1,0:T(8,128)(2,1)} %v_ref.3), custom_call_target="tpu_custom_call" | custom-call | flops 1 | bytes 1 | tf_op jit(solution)/shard_map/pallas_call | solution.py:347
  136.5 8.4 %collective-permute-done.11 = bf16[512,512]{1,0:T(8,128)(2,1)S(1)} collective-permute-done((bf16[512,512]{1,0:T(8,128)(2,1)}, bf16[512,512]{1,0:T(8,128)(2,1)S(1)}, u32[]{:S(2)}, u32[]{:S(2)}) %collective-permute-start.11) | collective-permute-done | bytes 524320 | tf_op jit(solution)/shard_map/ppermute | solution.py:40
  (61 shorter events, 9.2 us)
Async XLA Ops:
  2.6 24.2 %copy-start.8 = (bf16[1024,256]{1,0:T(8,128)(2,1)}, bf16[1024,256]{1,0:T(8,128)(2,1)S(1)}, u32[]{:S(2)}) copy-start(bf16[1024,256]{1,0:T(8,128)(2,1)S(1)} %constant_dynamic-update-slice_fusion.refs_3_) | copy-start | bytes 1572868
  2.7 22.7 %collective-permute-start = (bf16[1024,256]{1,0:T(8,128)(2,1)S(1)}, bf16[1024,256]{1,0:T(8,128)(2,1)S(1)}, u32[]{:S(2)}, u32[]{:S(2)}) collective-permute-start(bf16[1024,256]{1,0:T(8,128)(2,1)S(1)} %constant_dynamic-update-slice_fusion.refs_3_), channel_id=1, source_target_pairs={{0,16},{8,24},{16,32},{24,40},{32,48},{40,56},{48,0},{56,8},{64,80... | collective-permute-start | bytes 1572872 | tf_op jit(solution)/shard_map/ppermute | solution.py:40
  4.9 20.5 %collective-permute-start.1 = (bf16[1024,256]{1,0:T(8,128)(2,1)S(1)}, bf16[1024,256]{1,0:T(8,128)(2,1)S(1)}, u32[]{:S(2)}, u32[]{:S(2)}) collective-permute-start(bf16[1024,256]{1,0:T(8,128)(2,1)S(1)} %constant_dynamic-update-slice_fusion.refs_3_), channel_id=1, source_target_pairs={{0,48},{8,56},{16,0},{24,8},{32,16},{40,24},{48,32},{56,40},{64,11... | collective-permute-start | bytes 1572872 | tf_op jit(solution)/shard_map/ppermute | solution.py:40
  6.4 19.0 %collective-permute-start.2 = (bf16[1024,256]{1,0:T(8,128)(2,1)S(1)}, bf16[1024,256]{1,0:T(8,128)(2,1)S(1)}, u32[]{:S(2)}, u32[]{:S(2)}) collective-permute-start(bf16[1024,256]{1,0:T(8,128)(2,1)S(1)} %constant_dynamic-update-slice_fusion.refs_3_), channel_id=1, source_target_pairs={{0,64},{8,72},{16,80},{24,88},{32,96},{40,104},{48,112},{56,120},{... | collective-permute-start | bytes 1572872 | tf_op jit(solution)/shard_map/ppermute | solution.py:40
  10.7 16.1 %copy-start.12 = (bf16[2,8,4,128]{3,2,0,1:T(4,128)(2,1)}, bf16[2,8,4,128]{3,2,0,1:T(4,128)(2,1)S(1)}, u32[]{:S(2)}) copy-start(bf16[2,8,4,128]{3,2,0,1:T(4,128)(2,1)S(1)} %copy.18) | copy-start | bytes 49156
  25.4 1.5 %copy-start.5 = (bf16[1024,256]{1,0:T(8,128)(2,1)}, bf16[1024,256]{1,0:T(8,128)(2,1)S(1)}, u32[]{:S(2)}) copy-start(bf16[1024,256]{1,0:T(8,128)(2,1)S(1)} %collective-permute-done.1.refs_6_) | copy-start | bytes 1572868
  25.4 1.7 %copy-start.3 = (bf16[1024,256]{1,0:T(8,128)(2,1)}, bf16[1024,256]{1,0:T(8,128)(2,1)S(1)}, u32[]{:S(2)}) copy-start(bf16[1024,256]{1,0:T(8,128)(2,1)S(1)} %collective-permute-done.2.refs_7_) | copy-start | bytes 1572868
  26.8 6.0 %collective-permute-start.3 = (bf16[3072,256]{1,0:T(8,128)(2,1)}, bf16[3072,256]{1,0:T(8,128)(2,1)}, u32[]{:S(2)}, u32[]{:S(2)}) collective-permute-start(bf16[3072,256]{1,0:T(8,128)(2,1)} %pad_maximum_fusion), channel_id=1, source_target_pairs={{0,8},{8,0},{16,24},{24,16},{32,40},{40,32},{48,56},{56,48},{64,72... | collective-permute-start | bytes 4718600 | tf_op jit(solution)/shard_map/ppermute | solution.py:40
  26.9 4.2 %copy-start.14 = (s32[128]{0:T(128)S(1)}, s32[128]{0:T(128)}, u32[]{:S(2)}) copy-start(s32[128]{0:T(128)} %param.19) | copy-start | bytes 1540
  26.9 4.3 %copy-start.13 = (s32[128,16]{0,1:T(8,128)S(1)}, s32[128,16]{0,1:T(8,128)}, u32[]{:S(2)}) copy-start(s32[128,16]{0,1:T(8,128)} %param.18) | copy-start | bytes 24580
  28.4 20.2 %collective-permute-start.5 = (bf16[1536,256]{1,0:T(8,128)(2,1)}, bf16[1536,256]{1,0:T(8,128)(2,1)S(1)}, u32[]{:S(2)}, u32[]{:S(2)}) collective-permute-start(bf16[1536,256]{1,0:T(8,128)(2,1)} %get-tuple-element.35), channel_id=1, source_target_pairs={{0,16},{8,24},{16,32},{24,40},{32,48},{40,56},{48,0},{56,8},{64,80... | collective-permute-start | bytes 2359304 | tf_op jit(solution)/shard_map/ppermute | solution.py:40
  29.2 19.4 %collective-permute-start.6 = (bf16[1536,256]{1,0:T(8,128)(2,1)}, bf16[1536,256]{1,0:T(8,128)(2,1)S(1)}, u32[]{:S(2)}, u32[]{:S(2)}) collective-permute-start(bf16[1536,256]{1,0:T(8,128)(2,1)} %get-tuple-element.34), channel_id=1, source_target_pairs={{0,48},{8,56},{16,0},{24,8},{32,16},{40,24},{48,32},{56,40},{64,11... | collective-permute-start | bytes 2359304 | tf_op jit(solution)/shard_map/ppermute | solution.py:40
  32.8 11.5 %copy-start = (bf16[1024,512]{1,0:T(8,128)(2,1)S(1)}, bf16[1024,512]{1,0:T(8,128)(2,1)}, u32[]{:S(2)}) copy-start(bf16[1024,512]{1,0:T(8,128)(2,1)} %refs_1_.3) | copy-start | bytes 3145732
  45.2 6.0 %copy-start.9 = (bf16[1024,256]{1,0:T(8,128)(2,1)S(1)}, bf16[1024,256]{1,0:T(8,128)(2,1)}, u32[]{:S(2)}) copy-start(bf16[1024,256]{1,0:T(8,128)(2,1)} %copy-done.8) | copy-start | bytes 1572868
  48.6 8.3 %copy-start.1 = (bf16[1536,256]{1,0:T(8,128)(2,1)}, bf16[1536,256]{1,0:T(8,128)(2,1)S(1)}, u32[]{:S(2)}) copy-start(bf16[1536,256]{1,0:T(8,128)(2,1)S(1)} %collective-permute-done.5.refs_3_) | copy-start | bytes 2359300
  48.6 9.2 %copy-start.2 = (bf16[1536,256]{1,0:T(8,128)(2,1)}, bf16[1536,256]{1,0:T(8,128)(2,1)S(1)}, u32[]{:S(2)}) copy-start(bf16[1536,256]{1,0:T(8,128)(2,1)S(1)} %collective-permute-done.6.refs_4_) | copy-start | bytes 2359300
  50.0 51.5 %collective-permute-start.9 = (bf16[3072,256]{1,0:T(8,128)(2,1)}, bf16[3072,256]{1,0:T(8,128)(2,1)}, u32[]{:S(2)}, u32[]{:S(2)}) collective-permute-start(bf16[3072,256]{1,0:T(8,128)(2,1)} %pad_maximum_fusion.1), channel_id=1, source_target_pairs={{0,8},{8,0},{16,24},{24,16},{32,40},{40,32},{48,56},{56,48},{64,72... | collective-permute-start | bytes 4718600 | tf_op jit(solution)/shard_map/ppermute | solution.py:40
  51.2 14.7 %collective-permute-start.10 = (bf16[1024,256]{1,0:T(8,128)(2,1)S(1)}, bf16[1024,256]{1,0:T(8,128)(2,1)}, u32[]{:S(2)}, u32[]{:S(2)}) collective-permute-start(bf16[1024,256]{1,0:T(8,128)(2,1)S(1)} %copy-done.9), channel_id=1, source_target_pairs={{0,8},{8,0},{16,24},{24,16},{32,40},{40,32},{48,56},{56,48},{64,72... | collective-permute-start | bytes 1572872 | tf_op jit(solution)/shard_map/ppermute | solution.py:40
  51.2 18.4 %collective-permute-start.4 = (bf16[512,512]{1,0:T(8,128)(2,1)}, bf16[512,512]{1,0:T(8,128)(2,1)S(1)}, u32[]{:S(2)}, u32[]{:S(2)}) collective-permute-start(bf16[512,512]{1,0:T(8,128)(2,1)} %slice.15), channel_id=1, source_target_pairs={{0,120},{8,112},{16,104},{24,96},{32,88},{40,80},{48,72},{56,64},{... | collective-permute-start | bytes 1572872 | tf_op jit(solution)/shard_map/ppermute | solution.py:40
  58.6 42.9 %collective-permute-start.7 = (bf16[1024,256]{1,0:T(8,128)(2,1)}, bf16[1024,256]{1,0:T(8,128)(2,1)S(1)}, u32[]{:S(2)}, u32[]{:S(2)}) collective-permute-start(bf16[1024,256]{1,0:T(8,128)(2,1)} %slice.18), channel_id=1, source_target_pairs={{0,16},{8,24},{16,32},{24,40},{32,48},{40,56},{48,0},{56,8},{64,80... | collective-permute-start | bytes 1572872 | tf_op jit(solution)/shard_map/ppermute | solution.py:40
  58.6 42.9 %collective-permute-start.8 = (bf16[1024,256]{1,0:T(8,128)(2,1)}, bf16[1024,256]{1,0:T(8,128)(2,1)S(1)}, u32[]{:S(2)}, u32[]{:S(2)}) collective-permute-start(bf16[1024,256]{1,0:T(8,128)(2,1)} %slice.19), channel_id=1, source_target_pairs={{0,56},{8,48},{16,8},{24,0},{32,24},{40,16},{48,40},{56,32},{64,12... | collective-permute-start | bytes 1572872 | tf_op jit(solution)/shard_map/ppermute | solution.py:40
  61.5 40.0 %all-to-all-start.1 = ((bf16[128,16,128]{2,1,0:T(8,128)(2,1)}), bf16[128,16,128]{2,1,0:T(8,128)(2,1)S(1)}, u32[]{:S(2)}, u32[]{:S(2)}) async-start(bf16[128,16,128]{2,1,0:T(8,128)(2,1)} %shard_map.113), calls=%async_computation.1 | async-start | bytes 1048576 | tf_op jit(solution)/shard_map/all_to_all | solution.py:399
  101.5 25.9 %copy-start.7 = (bf16[128,16,128]{2,1,0:T(8,128)(2,1)}, bf16[128,16,128]{2,1,0:T(8,128)(2,1)S(1)}, u32[]{:S(2)}) copy-start(bf16[128,16,128]{2,1,0:T(8,128)(2,1)S(1)} %all-to-all-done.1) | copy-start | bytes 1572868
  127.4 17.5 %collective-permute-start.11 = (bf16[512,512]{1,0:T(8,128)(2,1)}, bf16[512,512]{1,0:T(8,128)(2,1)S(1)}, u32[]{:S(2)}, u32[]{:S(2)}) collective-permute-start(bf16[512,512]{1,0:T(8,128)(2,1)} %get-tuple-element.30), channel_id=1, source_target_pairs={{0,120},{8,112},{16,104},{24,96},{32,88},{40,80},{48,72},{56,64},{... | collective-permute-start | bytes 1572872 | tf_op jit(solution)/shard_map/ppermute | solution.py:40
  (4 other events, 4.2 us)

commit v3 on v2

--- a/solution.py
+++ b/solution.py
@@ -20,6 +20,7 @@
 SMEM = pl.BlockSpec(memory_space=pltpu.SMEM)
 ANY = pl.BlockSpec(memory_space=pl.ANY)
 TINY = pl.CostEstimate(flops=1, bytes_accessed=1, transcendentals=0)
+LONG = pl.CostEstimate(flops=1 << 35, bytes_accessed=1 << 24, transcendentals=1 << 24)
 NT = (((1,), (1,)), ((), ()))
 
 
@@ -223,7 +224,7 @@
             *[pltpu.VMEM(part.shape, jnp.float32) for part in state or []],
         ],
         compiler_params=pltpu.CompilerParams(vmem_limit_bytes=58 << 20),
-        cost_estimate=TINY,
+        cost_estimate=TINY if final else LONG,
     )(*operands)
 
 
@@ -431,7 +432,7 @@
     near_sources += [(5, k * KEYS, KEYS, 5 + k, 0) for k in range(3)]
     mirror_slot = jnp.where(y % 2 == 0, 5, 6)
     numbers = jnp.stack([*near_ids, *far_ids, me, 15 - me, mirror_slot]).astype(jnp.int32)
-    own = after([own], [parts])[0]
+    numbers = after([numbers], [parts])[0]
     state = flash(
         numbers,
         queries,

time: 146 us -> 144 us (0.986)
  starting transfers between devices: 28.8 us -> 24.9 us
  waiting for transfers between devices: 15.6 us -> 18.4 us
    ppermute x12, starting transfers between devices: 25.2 us -> 20.8 us  [permute(): return lax.ppermute(value, 'inst', pairs)]
    ppermute x12, waiting for transfers between devices: 15.6 us -> 18.4 us  [permute(): return lax.ppermute(value, 'inst', pairs)]
    unnamed x32 -> x26, local copies, waits for them, and re-layouts: 3.1 us -> 2.9 us
  transfers between devices with their start and end apart: 13 -> 13, of which waited for: 3 -> 2; matrix products, arithmetic and copies ran while one was open for 6% -> 6% of each run, Pallas kernels for 31% -> 31%
where the time goes in v3:
time: 144 us; the launch traced here: 143 us
  Pallas kernels  69.7 us (48%)
  starting transfers between devices  24.9 us (17%)
  waiting for transfers between devices  18.4 us (13%)
  blocking collectives  14.9 us (10%)
  local copies, waits for them, and re-layouts  9.32 us (6%)
  other arithmetic  5.38 us (4%)
    pallas_call x2, Pallas kernels, flash(): pl.pallas_call(functools.partial(flash_kernel, half_count, sources, state...  55.9 us
    ppermute x12, starting transfers between devices, permute(): return lax.ppermute(value, 'inst', pairs)  20.8 us
    ppermute x12, waiting for transfers between devices, permute(): return lax.ppermute(value, 'inst', pairs)  18.4 us
    all_to_all x1, blocking collectives, body(): every_query = lax.all_to_all(copies, 'inst', 0, 0, tiled=True)  14.9 us
    pallas_call x1, Pallas kernels, decode_cache(): pl.pallas_call(decode_kernel, out_shape=jax.ShapeDtypeStruct((req_count,...  11.5 us
    all_to_all x1, starting transfers between devices, body(): received = lax.all_to_all(parts, 'inst', 0, 0, tiled=True)  4.11 us
    unnamed x26, local copies, waits for them, and re-layouts  2.9 us
  transfers between devices with their start and end apart: 13, of which 2 were waited for; matrix products, arithmetic and copies ran while one was open for 6% of the time, Pallas kernels for 31%

profile of v3, /device:TPU:1, one launch (start us, length us, event | category | flops | bytes accessed | tf_op | source)
XLA Modules:
  0.0 143.4 jit_solution(12434260921782273587)
XLA Ops:
  0.6 1.7 %constant_dynamic-update-slice_fusion.1 = bf16[1024,256]{1,0:T(8,128)(2,1)} fusion(bf16[1024,128]{1,0:T(8,128)(2,1)} %param.11), kind=kLoop, calls=%fused_computation.11 | loop fusion | bytes 524288
  2.3 1.7 %constant_dynamic-update-slice_fusion.refs_3_ = bf16[1024,256]{1,0:T(8,128)(2,1)} fusion(bf16[1024,256]{1,0:T(8,128)(2,1)} %constant_dynamic-update-slice_fusion.1, bf16[1024,128]{1,0:T(8,128)(2,1)} %param.12), kind=kLoop, calls=%fused_computation.10 | loop fusion | bytes 524288 | tf_op jit(solution)/shard_map/concatenate | solution.py:378
  4.0 2.1 %collective-permute-start = (bf16[1024,256]{1,0:T(8,128)(2,1)}, bf16[1024,256]{1,0:T(8,128)(2,1)S(1)}, u32[]{:S(2)}, u32[]{:S(2)}) collective-permute-start(bf16[1024,256]{1,0:T(8,128)(2,1)} %constant_dynamic-update-slice_fusion.refs_3_), channel_id=1, source_target_pairs={{0,16},{8,24},{16,32},{24,40},{32,48},{40,56},{48,0},{56,8},{64,80... | collective-permute-start | bytes 1572872 | tf_op jit(solution)/shard_map/ppermute | solution.py:41
  6.1 1.4 %collective-permute-start.1 = (bf16[1024,256]{1,0:T(8,128)(2,1)}, bf16[1024,256]{1,0:T(8,128)(2,1)S(1)}, u32[]{:S(2)}, u32[]{:S(2)}) collective-permute-start(bf16[1024,256]{1,0:T(8,128)(2,1)} %constant_dynamic-update-slice_fusion.refs_3_), channel_id=1, source_target_pairs={{0,48},{8,56},{16,0},{24,8},{32,16},{40,24},{48,32},{56,40},{64,11... | collective-permute-start | bytes 1572872 | tf_op jit(solution)/shard_map/ppermute | solution.py:41
  7.6 3.6 %collective-permute-start.2 = (bf16[1024,256]{1,0:T(8,128)(2,1)}, bf16[1024,256]{1,0:T(8,128)(2,1)S(1)}, u32[]{:S(2)}, u32[]{:S(2)}) collective-permute-start(bf16[1024,256]{1,0:T(8,128)(2,1)} %constant_dynamic-update-slice_fusion.refs_3_), channel_id=1, source_target_pairs={{0,64},{8,72},{16,80},{24,88},{32,96},{40,104},{48,112},{56,120},{... | collective-permute-start | bytes 1572872 | tf_op jit(solution)/shard_map/ppermute | solution.py:41
  11.9 14.9 %all_to_all.10.q_ref = bf16[128,8,128]{2,1,0:T(8,128)(2,1)} all-to-all(bf16[128,8,128]{2,1,0:T(8,128)(2,1)S(1)} %bitcast.28), channel_id=1, replica_groups=mesh['inst'=16,'tp'=8] {'inst'}, dimensions={0} | all-to-all | bytes 524288 | tf_op jit(solution)/shard_map/all_to_all | solution.py:376
  26.9 1.4 pad_maximum_fusion
  28.9 1.0 pad_maximum_fusion.2
  29.8 0.9 collective-permute-start.5
  30.7 1.8 %collective-permute-start.6 = (bf16[1536,256]{1,0:T(8,128)(2,1)S(1)}, bf16[1536,256]{1,0:T(8,128)(2,1)S(1)}, u32[]{:S(2)}, u32[]{:S(2)}) collective-permute-start(bf16[1536,256]{1,0:T(8,128)(2,1)S(1)} %get-tuple-element.34), channel_id=1, source_target_pairs={{0,48},{8,56},{16,0},{24,8},{32,16},{40,24},{48,32},{56,40},{64,11... | collective-permute-start | bytes 2359304 | tf_op jit(solution)/shard_map/ppermute | solution.py:41
  32.9 0.9 fusion.1
  34.3 11.5 %shard_map.113 = bf16[128,16,128]{2,1,0:T(8,128)(2,1)} custom-call(s32[128]{0:T(128)} %and_select_fusion.owner, s32[128]{0:T(128)} %get-tuple-element.32.live, bf16[128,8,128]{2,1,0:T(8,128)(2,1)} %all_to_all.10.q_ref, bf16[128,128,128]{2,1,0:T(8,128)(2,1)} %k_ref.2, bf16[128,128,128]{2,1,0:T(8,128)(2,1)} %v_ref.2), custom_call_target="tpu_custom_call" | custom-call | flops 1 | bytes 1 | tf_op jit(solution)/shard_map/pallas_call | solution.py:301
  45.8 0.8 slice.15
  46.6 3.5 %collective-permute-start.4 = (bf16[512,512]{1,0:T(8,128)(2,1)}, bf16[512,512]{1,0:T(8,128)(2,1)}, u32[]{:S(2)}, u32[]{:S(2)}) collective-permute-start(bf16[512,512]{1,0:T(8,128)(2,1)} %slice.15), channel_id=1, source_target_pairs={{0,120},{8,112},{16,104},{24,96},{32,88},{40,80},{48,72},{56,64},{... | collective-permute-start | bytes 1572872 | tf_op jit(solution)/shard_map/ppermute | solution.py:41
  50.9 4.1 %all-to-all-start.1 = ((bf16[128,16,128]{2,1,0:T(8,128)(2,1)}), bf16[128,16,128]{2,1,0:T(8,128)(2,1)S(1)}, u32[]{:S(2)}, u32[]{:S(2)}) async-start(bf16[128,16,128]{2,1,0:T(8,128)(2,1)} %shard_map.113), calls=%async_computation.1 | async-start | bytes 1048576 | tf_op jit(solution)/shard_map/all_to_all | solution.py:400
  55.1 1.5 %pad_maximum_fusion.1 = bf16[3072,256]{1,0:T(8,128)(2,1)} fusion(bf16[1536,256]{1,0:T(8,128)(2,1)S(1)} %collective-permute-done.6.refs_4_, bf16[1536,256]{1,0:T(8,128)(2,1)S(1)} %collective-permute-done.5.refs_3_), kind=kLoop, calls=%fused_computation.1 | loop fusion | flops 3145728 | bytes 3145728 | tf_op jit(solution)/shard_map/concatenate | solution.py:409
  56.8 1.6 %collective-permute-start.7 = (bf16[1024,256]{1,0:T(8,128)(2,1)S(1)}, bf16[1024,256]{1,0:T(8,128)(2,1)S(1)}, u32[]{:S(2)}, u32[]{:S(2)}) collective-permute-start(bf16[1024,256]{1,0:T(8,128)(2,1)S(1)} %slice.18), channel_id=1, source_target_pairs={{0,16},{8,24},{16,32},{24,40},{32,48},{40,56},{48,0},{56,8},{64,80... | collective-permute-start | bytes 1572872 | tf_op jit(solution)/shard_map/ppermute | solution.py:41
  58.4 1.6 %collective-permute-start.8 = (bf16[1024,256]{1,0:T(8,128)(2,1)S(1)}, bf16[1024,256]{1,0:T(8,128)(2,1)S(1)}, u32[]{:S(2)}, u32[]{:S(2)}) collective-permute-start(bf16[1024,256]{1,0:T(8,128)(2,1)S(1)} %slice.19), channel_id=1, source_target_pairs={{0,56},{8,48},{16,8},{24,0},{32,24},{40,16},{48,40},{56,32},{64,12... | collective-permute-start | bytes 1572872 | tf_op jit(solution)/shard_map/ppermute | solution.py:41
  60.0 7.7 %collective-permute-done.4.refs_2_ = bf16[512,512]{1,0:T(8,128)(2,1)} collective-permute-done((bf16[512,512]{1,0:T(8,128)(2,1)}, bf16[512,512]{1,0:T(8,128)(2,1)}, u32[]{:S(2)}, u32[]{:S(2)}) %collective-permute-start.4) | collective-permute-done | bytes 524320 | tf_op jit(solution)/shard_map/ppermute | solution.py:41
  67.7 31.1 %shard_map.114 = (f32[2,4,512,128]{3,2,1,0:T(8,128)}, f32[2,4,512,128]{3,2,1,0:T(8,128)}) custom-call(s32[19]{0:T(128)} %stack.76.refs_0_, bf16[1024,512]{1,0:T(8,128)(2,1)} %refs_1_.3, bf16[512,512]{1,0:T(8,128)(2,1)} %collective-permute-done.4.refs_2_, bf16[1024,256]{1,0:T(8,128)(2,1)} %constant_dynamic-update-slice_fusion.refs_3_, ...), custom_call_target="tpu_custom_call" | custom-call | flops 34359738368 | bytes 16777216 | tf_op jit(solution)/shard_map/pallas_call | solution.py:208
  99.9 24.8 %shard_map.115 = (bf16[1024,512]{1,0:T(8,128)(2,1)}, bf16[512,512]{1,0:T(8,128)(2,1)}) custom-call(s32[19]{0:T(128)} %stack.76.refs_0_, bf16[1024,512]{1,0:T(8,128)(2,1)} %refs_1_.3, bf16[512,512]{1,0:T(8,128)(2,1)} %collective-permute-done.4.refs_2_, bf16[1536,256]{1,0:T(8,128)(2,1)} %copy-done, bf16[1536,256]{1,0:T(8,128)(2,1)} %copy-done.1, ...), custom_call_target="tpu_custom_call" | custom-call | flops 1 | bytes 1 | tf_op jit(solution)/shard_map/pallas_call | solution.py:208
  124.7 3.6 %collective-permute-start.11 = (bf16[512,512]{1,0:T(8,128)(2,1)}, bf16[512,512]{1,0:T(8,128)(2,1)S(1)}, u32[]{:S(2)}, u32[]{:S(2)}) collective-permute-start(bf16[512,512]{1,0:T(8,128)(2,1)} %get-tuple-element.30), channel_id=1, source_target_pairs={{0,120},{8,112},{16,104},{24,96},{32,88},{40,80},{48,72},{56,64},{... | collective-permute-start | bytes 1572872 | tf_op jit(solution)/shard_map/ppermute | solution.py:41
  128.2 2.3 %shard_map.116 = bf16[8,8,128]{2,1,0:T(8,128)(2,1)} custom-call(bf16[16,8,16,128]{3,2,1,0:T(8,128)(2,1)} %bitcast.27, bf16[8,8,128]{2,1,0:T(8,128)(2,1)} %bitcast.30, bf16[2,8,128]{2,1,0:T(8,128)(2,1)} %k_ref.3, bf16[2,8,128]{2,1,0:T(8,128)(2,1)} %v_ref.3), custom_call_target="tpu_custom_call" | custom-call | flops 1 | bytes 1 | tf_op jit(solution)/shard_map/pallas_call | solution.py:348
  131.9 10.7 %collective-permute-done.11 = bf16[512,512]{1,0:T(8,128)(2,1)S(1)} collective-permute-done((bf16[512,512]{1,0:T(8,128)(2,1)}, bf16[512,512]{1,0:T(8,128)(2,1)S(1)}, u32[]{:S(2)}, u32[]{:S(2)}) %collective-permute-start.11) | collective-permute-done | bytes 524320 | tf_op jit(solution)/shard_map/ppermute | solution.py:41
  (55 shorter events, 6.4 us)
Async XLA Ops:
  4.0 22.8 %collective-permute-start = (bf16[1024,256]{1,0:T(8,128)(2,1)}, bf16[1024,256]{1,0:T(8,128)(2,1)S(1)}, u32[]{:S(2)}, u32[]{:S(2)}) collective-permute-start(bf16[1024,256]{1,0:T(8,128)(2,1)} %constant_dynamic-update-slice_fusion.refs_3_), channel_id=1, source_target_pairs={{0,16},{8,24},{16,32},{24,40},{32,48},{40,56},{48,0},{56,8},{64,80... | collective-permute-start | bytes 1572872 | tf_op jit(solution)/shard_map/ppermute | solution.py:41
  6.1 20.7 %collective-permute-start.1 = (bf16[1024,256]{1,0:T(8,128)(2,1)}, bf16[1024,256]{1,0:T(8,128)(2,1)S(1)}, u32[]{:S(2)}, u32[]{:S(2)}) collective-permute-start(bf16[1024,256]{1,0:T(8,128)(2,1)} %constant_dynamic-update-slice_fusion.refs_3_), channel_id=1, source_target_pairs={{0,48},{8,56},{16,0},{24,8},{32,16},{40,24},{48,32},{56,40},{64,11... | collective-permute-start | bytes 1572872 | tf_op jit(solution)/shard_map/ppermute | solution.py:41
  7.6 19.3 %collective-permute-start.2 = (bf16[1024,256]{1,0:T(8,128)(2,1)}, bf16[1024,256]{1,0:T(8,128)(2,1)S(1)}, u32[]{:S(2)}, u32[]{:S(2)}) collective-permute-start(bf16[1024,256]{1,0:T(8,128)(2,1)} %constant_dynamic-update-slice_fusion.refs_3_), channel_id=1, source_target_pairs={{0,64},{8,72},{16,80},{24,88},{32,96},{40,104},{48,112},{56,120},{... | collective-permute-start | bytes 1572872 | tf_op jit(solution)/shard_map/ppermute | solution.py:41
  11.9 16.4 %copy-start.9 = (bf16[2,8,4,128]{3,2,0,1:T(4,128)(2,1)}, bf16[2,8,4,128]{3,2,0,1:T(4,128)(2,1)S(1)}, u32[]{:S(2)}) copy-start(bf16[2,8,4,128]{3,2,0,1:T(4,128)(2,1)S(1)} %copy.18) | copy-start | bytes 49156
  26.8 1.9 %copy-start.5 = (bf16[1024,256]{1,0:T(8,128)(2,1)}, bf16[1024,256]{1,0:T(8,128)(2,1)S(1)}, u32[]{:S(2)}) copy-start(bf16[1024,256]{1,0:T(8,128)(2,1)S(1)} %collective-permute-done.refs_5_) | copy-start | bytes 1572868
  26.8 1.9 %copy-start.6 = (bf16[1024,256]{1,0:T(8,128)(2,1)}, bf16[1024,256]{1,0:T(8,128)(2,1)S(1)}, u32[]{:S(2)}) copy-start(bf16[1024,256]{1,0:T(8,128)(2,1)S(1)} %collective-permute-done.1.refs_6_) | copy-start | bytes 1572868
  26.9 2.0 %copy-start.3 = (bf16[1024,256]{1,0:T(8,128)(2,1)}, bf16[1024,256]{1,0:T(8,128)(2,1)S(1)}, u32[]{:S(2)}) copy-start(bf16[1024,256]{1,0:T(8,128)(2,1)S(1)} %collective-permute-done.2.refs_7_) | copy-start | bytes 1572868
  28.3 6.1 %collective-permute-start.3 = (bf16[3072,256]{1,0:T(8,128)(2,1)}, bf16[3072,256]{1,0:T(8,128)(2,1)}, u32[]{:S(2)}, u32[]{:S(2)}) collective-permute-start(bf16[3072,256]{1,0:T(8,128)(2,1)} %pad_maximum_fusion), channel_id=1, source_target_pairs={{0,8},{8,0},{16,24},{24,16},{32,40},{40,32},{48,56},{56,48},{64,72... | collective-permute-start | bytes 4718600 | tf_op jit(solution)/shard_map/ppermute | solution.py:41
  28.3 31.8 %collective-permute-start.10 = (bf16[1024,256]{1,0:T(8,128)(2,1)}, bf16[1024,256]{1,0:T(8,128)(2,1)}, u32[]{:S(2)}, u32[]{:S(2)}) collective-permute-start(bf16[1024,256]{1,0:T(8,128)(2,1)} %constant_dynamic-update-slice_fusion.refs_3_), channel_id=1, source_target_pairs={{0,8},{8,0},{16,24},{24,16},{32,40},{40,32},{48,56},{56,48},{64,72... | collective-permute-start | bytes 1572872 | tf_op jit(solution)/shard_map/ppermute | solution.py:41
  28.8 3.7 %copy-start.11 = (s32[128]{0:T(128)S(1)}, s32[128]{0:T(128)}, u32[]{:S(2)}) copy-start(s32[128]{0:T(128)} %param.19) | copy-start | bytes 1540
  28.8 3.9 %copy-start.10 = (s32[128,16]{0,1:T(8,128)S(1)}, s32[128,16]{0,1:T(8,128)}, u32[]{:S(2)}) copy-start(s32[128,16]{0,1:T(8,128)} %param.18) | copy-start | bytes 24580
  29.8 25.1 %collective-permute-start.5 = (bf16[1536,256]{1,0:T(8,128)(2,1)}, bf16[1536,256]{1,0:T(8,128)(2,1)S(1)}, u32[]{:S(2)}, u32[]{:S(2)}) collective-permute-start(bf16[1536,256]{1,0:T(8,128)(2,1)} %get-tuple-element.35), channel_id=1, source_target_pairs={{0,16},{8,24},{16,32},{24,40},{32,48},{40,56},{48,0},{56,8},{64,80... | collective-permute-start | bytes 2359304 | tf_op jit(solution)/shard_map/ppermute | solution.py:41
  30.7 24.3 %collective-permute-start.6 = (bf16[1536,256]{1,0:T(8,128)(2,1)S(1)}, bf16[1536,256]{1,0:T(8,128)(2,1)S(1)}, u32[]{:S(2)}, u32[]{:S(2)}) collective-permute-start(bf16[1536,256]{1,0:T(8,128)(2,1)S(1)} %get-tuple-element.34), channel_id=1, source_target_pairs={{0,48},{8,56},{16,0},{24,8},{32,16},{40,24},{48,32},{56,40},{64,11... | collective-permute-start | bytes 2359304 | tf_op jit(solution)/shard_map/ppermute | solution.py:41
  34.3 11.5 %copy-start.2 = (bf16[1024,512]{1,0:T(8,128)(2,1)S(1)}, bf16[1024,512]{1,0:T(8,128)(2,1)}, u32[]{:S(2)}) copy-start(bf16[1024,512]{1,0:T(8,128)(2,1)} %refs_1_.3) | copy-start | bytes 3145732
  46.6 21.1 %collective-permute-start.4 = (bf16[512,512]{1,0:T(8,128)(2,1)}, bf16[512,512]{1,0:T(8,128)(2,1)}, u32[]{:S(2)}, u32[]{:S(2)}) collective-permute-start(bf16[512,512]{1,0:T(8,128)(2,1)} %slice.15), channel_id=1, source_target_pairs={{0,120},{8,112},{16,104},{24,96},{32,88},{40,80},{48,72},{56,64},{... | collective-permute-start | bytes 1572872 | tf_op jit(solution)/shard_map/ppermute | solution.py:41
  50.9 48.0 %all-to-all-start.1 = ((bf16[128,16,128]{2,1,0:T(8,128)(2,1)}), bf16[128,16,128]{2,1,0:T(8,128)(2,1)S(1)}, u32[]{:S(2)}, u32[]{:S(2)}) async-start(bf16[128,16,128]{2,1,0:T(8,128)(2,1)} %shard_map.113), calls=%async_computation.1 | async-start | bytes 1048576 | tf_op jit(solution)/shard_map/all_to_all | solution.py:400
  55.0 1.6 %copy-start = (bf16[1536,256]{1,0:T(8,128)(2,1)}, bf16[1536,256]{1,0:T(8,128)(2,1)S(1)}, u32[]{:S(2)}) copy-start(bf16[1536,256]{1,0:T(8,128)(2,1)S(1)} %collective-permute-done.5.refs_3_) | copy-start | bytes 2359300
  55.0 1.7 %copy-start.1 = (bf16[1536,256]{1,0:T(8,128)(2,1)}, bf16[1536,256]{1,0:T(8,128)(2,1)S(1)}, u32[]{:S(2)}) copy-start(bf16[1536,256]{1,0:T(8,128)(2,1)S(1)} %collective-permute-done.6.refs_4_) | copy-start | bytes 2359300
  56.7 42.2 %collective-permute-start.9 = (bf16[3072,256]{1,0:T(8,128)(2,1)}, bf16[3072,256]{1,0:T(8,128)(2,1)}, u32[]{:S(2)}, u32[]{:S(2)}) collective-permute-start(bf16[3072,256]{1,0:T(8,128)(2,1)} %pad_maximum_fusion.1), channel_id=1, source_target_pairs={{0,8},{8,0},{16,24},{24,16},{32,40},{40,32},{48,56},{56,48},{64,72... | collective-permute-start | bytes 4718600 | tf_op jit(solution)/shard_map/ppermute | solution.py:41
  56.8 42.1 %collective-permute-start.7 = (bf16[1024,256]{1,0:T(8,128)(2,1)S(1)}, bf16[1024,256]{1,0:T(8,128)(2,1)S(1)}, u32[]{:S(2)}, u32[]{:S(2)}) collective-permute-start(bf16[1024,256]{1,0:T(8,128)(2,1)S(1)} %slice.18), channel_id=1, source_target_pairs={{0,16},{8,24},{16,32},{24,40},{32,48},{40,56},{48,0},{56,8},{64,80... | collective-permute-start | bytes 1572872 | tf_op jit(solution)/shard_map/ppermute | solution.py:41
  58.4 40.4 %collective-permute-start.8 = (bf16[1024,256]{1,0:T(8,128)(2,1)S(1)}, bf16[1024,256]{1,0:T(8,128)(2,1)S(1)}, u32[]{:S(2)}, u32[]{:S(2)}) collective-permute-start(bf16[1024,256]{1,0:T(8,128)(2,1)S(1)} %slice.19), channel_id=1, source_target_pairs={{0,56},{8,48},{16,8},{24,0},{32,24},{40,16},{48,40},{56,32},{64,12... | collective-permute-start | bytes 1572872 | tf_op jit(solution)/shard_map/ppermute | solution.py:41
  98.8 25.9 %copy-start.4 = (bf16[128,16,128]{2,1,0:T(8,128)(2,1)}, bf16[128,16,128]{2,1,0:T(8,128)(2,1)S(1)}, u32[]{:S(2)}) copy-start(bf16[128,16,128]{2,1,0:T(8,128)(2,1)S(1)} %all-to-all-done.1) | copy-start | bytes 1572868
  98.9 1.0 copy-start.8
  124.7 17.9 %collective-permute-start.11 = (bf16[512,512]{1,0:T(8,128)(2,1)}, bf16[512,512]{1,0:T(8,128)(2,1)S(1)}, u32[]{:S(2)}, u32[]{:S(2)}) collective-permute-start(bf16[512,512]{1,0:T(8,128)(2,1)} %get-tuple-element.30), channel_id=1, source_target_pairs={{0,120},{8,112},{16,104},{24,96},{32,88},{40,80},{48,72},{56,64},{... | collective-permute-start | bytes 1572872 | tf_op jit(solution)/shard_map/ppermute | solution.py:41
  (1 other events, 0.8 us)

commit v4 on v3

--- a/solution.py
+++ b/solution.py
@@ -432,7 +432,7 @@
     near_sources += [(5, k * KEYS, KEYS, 5 + k, 0) for k in range(3)]
     mirror_slot = jnp.where(y % 2 == 0, 5, 6)
     numbers = jnp.stack([*near_ids, *far_ids, me, 15 - me, mirror_slot]).astype(jnp.int32)
-    numbers = after([numbers], [parts])[0]
+    own = after([own], [parts])[0]
     state = flash(
         numbers,
         queries,

time: 144 us -> 144 us (level)
  no operation moved by 1% of the time
where the time goes in v4:
time: 144 us; the launch traced here: 143 us
  Pallas kernels  69.7 us (48%)
  starting transfers between devices  24.9 us (17%)
  waiting for transfers between devices  18.4 us (13%)
  blocking collectives  14.9 us (10%)
  local copies, waits for them, and re-layouts  9.32 us (6%)
  other arithmetic  5.38 us (4%)
    pallas_call x2, Pallas kernels, flash(): pl.pallas_call(functools.partial(flash_kernel, half_count, sources, state...  55.9 us
    ppermute x12, starting transfers between devices, permute(): return lax.ppermute(value, 'inst', pairs)  20.8 us
    ppermute x12, waiting for transfers between devices, permute(): return lax.ppermute(value, 'inst', pairs)  18.4 us
    all_to_all x1, blocking collectives, body(): every_query = lax.all_to_all(copies, 'inst', 0, 0, tiled=True)  14.9 us
    pallas_call x1, Pallas kernels, decode_cache(): pl.pallas_call(decode_kernel, out_shape=jax.ShapeDtypeStruct((req_count,...  11.5 us
    all_to_all x1, starting transfers between devices, body(): received = lax.all_to_all(parts, 'inst', 0, 0, tiled=True)  4.11 us
    unnamed x26, local copies, waits for them, and re-layouts  2.9 us
  transfers between devices with their start and end apart: 13, of which 2 were waited for; matrix products, arithmetic and copies ran while one was open for 6% of the time, Pallas kernels for 31%

profile of v4, /device:TPU:1, one launch (start us, length us, event | category | flops | bytes accessed | tf_op | source)
XLA Modules:
  0.0 143.4 jit_solution(12434260921782273587)
XLA Ops:
  0.6 1.7 %constant_dynamic-update-slice_fusion.1 = bf16[1024,256]{1,0:T(8,128)(2,1)} fusion(bf16[1024,128]{1,0:T(8,128)(2,1)} %param.11), kind=kLoop, calls=%fused_computation.11 | loop fusion | bytes 524288
  2.3 1.7 %constant_dynamic-update-slice_fusion.refs_3_ = bf16[1024,256]{1,0:T(8,128)(2,1)} fusion(bf16[1024,256]{1,0:T(8,128)(2,1)} %constant_dynamic-update-slice_fusion.1, bf16[1024,128]{1,0:T(8,128)(2,1)} %param.12), kind=kLoop, calls=%fused_computation.10 | loop fusion | bytes 524288 | tf_op jit(solution)/shard_map/concatenate | solution.py:378
  4.0 2.1 %collective-permute-start = (bf16[1024,256]{1,0:T(8,128)(2,1)}, bf16[1024,256]{1,0:T(8,128)(2,1)S(1)}, u32[]{:S(2)}, u32[]{:S(2)}) collective-permute-start(bf16[1024,256]{1,0:T(8,128)(2,1)} %constant_dynamic-update-slice_fusion.refs_3_), channel_id=1, source_target_pairs={{0,16},{8,24},{16,32},{24,40},{32,48},{40,56},{48,0},{56,8},{64,80... | collective-permute-start | bytes 1572872 | tf_op jit(solution)/shard_map/ppermute | solution.py:41
  6.1 1.4 %collective-permute-start.1 = (bf16[1024,256]{1,0:T(8,128)(2,1)}, bf16[1024,256]{1,0:T(8,128)(2,1)S(1)}, u32[]{:S(2)}, u32[]{:S(2)}) collective-permute-start(bf16[1024,256]{1,0:T(8,128)(2,1)} %constant_dynamic-update-slice_fusion.refs_3_), channel_id=1, source_target_pairs={{0,48},{8,56},{16,0},{24,8},{32,16},{40,24},{48,32},{56,40},{64,11... | collective-permute-start | bytes 1572872 | tf_op jit(solution)/shard_map/ppermute | solution.py:41
  7.6 3.6 %collective-permute-start.2 = (bf16[1024,256]{1,0:T(8,128)(2,1)}, bf16[1024,256]{1,0:T(8,128)(2,1)S(1)}, u32[]{:S(2)}, u32[]{:S(2)}) collective-permute-start(bf16[1024,256]{1,0:T(8,128)(2,1)} %constant_dynamic-update-slice_fusion.refs_3_), channel_id=1, source_target_pairs={{0,64},{8,72},{16,80},{24,88},{32,96},{40,104},{48,112},{56,120},{... | collective-permute-start | bytes 1572872 | tf_op jit(solution)/shard_map/ppermute | solution.py:41
  11.9 14.9 %all_to_all.10.q_ref = bf16[128,8,128]{2,1,0:T(8,128)(2,1)} all-to-all(bf16[128,8,128]{2,1,0:T(8,128)(2,1)S(1)} %bitcast.28), channel_id=1, replica_groups=mesh['inst'=16,'tp'=8] {'inst'}, dimensions={0} | all-to-all | bytes 524288 | tf_op jit(solution)/shard_map/all_to_all | solution.py:376
  26.9 1.4 pad_maximum_fusion
  28.9 1.0 pad_maximum_fusion.2
  29.8 0.9 collective-permute-start.5
  30.7 1.8 %collective-permute-start.6 = (bf16[1536,256]{1,0:T(8,128)(2,1)S(1)}, bf16[1536,256]{1,0:T(8,128)(2,1)S(1)}, u32[]{:S(2)}, u32[]{:S(2)}) collective-permute-start(bf16[1536,256]{1,0:T(8,128)(2,1)S(1)} %get-tuple-element.34), channel_id=1, source_target_pairs={{0,48},{8,56},{16,0},{24,8},{32,16},{40,24},{48,32},{56,40},{64,11... | collective-permute-start | bytes 2359304 | tf_op jit(solution)/shard_map/ppermute | solution.py:41
  32.9 0.9 fusion.1
  34.3 11.5 %shard_map.113 = bf16[128,16,128]{2,1,0:T(8,128)(2,1)} custom-call(s32[128]{0:T(128)} %and_select_fusion.owner, s32[128]{0:T(128)} %get-tuple-element.32.live, bf16[128,8,128]{2,1,0:T(8,128)(2,1)} %all_to_all.10.q_ref, bf16[128,128,128]{2,1,0:T(8,128)(2,1)} %k_ref.2, bf16[128,128,128]{2,1,0:T(8,128)(2,1)} %v_ref.2), custom_call_target="tpu_custom_call" | custom-call | flops 1 | bytes 1 | tf_op jit(solution)/shard_map/pallas_call | solution.py:301
  45.8 0.8 slice.15
  46.6 3.5 %collective-permute-start.4 = (bf16[512,512]{1,0:T(8,128)(2,1)}, bf16[512,512]{1,0:T(8,128)(2,1)}, u32[]{:S(2)}, u32[]{:S(2)}) collective-permute-start(bf16[512,512]{1,0:T(8,128)(2,1)} %slice.15), channel_id=1, source_target_pairs={{0,120},{8,112},{16,104},{24,96},{32,88},{40,80},{48,72},{56,64},{... | collective-permute-start | bytes 1572872 | tf_op jit(solution)/shard_map/ppermute | solution.py:41
  50.9 4.1 %all-to-all-start.1 = ((bf16[128,16,128]{2,1,0:T(8,128)(2,1)}), bf16[128,16,128]{2,1,0:T(8,128)(2,1)S(1)}, u32[]{:S(2)}, u32[]{:S(2)}) async-start(bf16[128,16,128]{2,1,0:T(8,128)(2,1)} %shard_map.113), calls=%async_computation.1 | async-start | bytes 1048576 | tf_op jit(solution)/shard_map/all_to_all | solution.py:400
  55.1 1.5 %pad_maximum_fusion.1 = bf16[3072,256]{1,0:T(8,128)(2,1)} fusion(bf16[1536,256]{1,0:T(8,128)(2,1)S(1)} %collective-permute-done.6.refs_4_, bf16[1536,256]{1,0:T(8,128)(2,1)S(1)} %collective-permute-done.5.refs_3_), kind=kLoop, calls=%fused_computation.1 | loop fusion | flops 3145728 | bytes 3145728 | tf_op jit(solution)/shard_map/concatenate | solution.py:409
  56.8 1.6 %collective-permute-start.7 = (bf16[1024,256]{1,0:T(8,128)(2,1)S(1)}, bf16[1024,256]{1,0:T(8,128)(2,1)S(1)}, u32[]{:S(2)}, u32[]{:S(2)}) collective-permute-start(bf16[1024,256]{1,0:T(8,128)(2,1)S(1)} %slice.18), channel_id=1, source_target_pairs={{0,16},{8,24},{16,32},{24,40},{32,48},{40,56},{48,0},{56,8},{64,80... | collective-permute-start | bytes 1572872 | tf_op jit(solution)/shard_map/ppermute | solution.py:41
  58.4 1.6 %collective-permute-start.8 = (bf16[1024,256]{1,0:T(8,128)(2,1)S(1)}, bf16[1024,256]{1,0:T(8,128)(2,1)S(1)}, u32[]{:S(2)}, u32[]{:S(2)}) collective-permute-start(bf16[1024,256]{1,0:T(8,128)(2,1)S(1)} %slice.19), channel_id=1, source_target_pairs={{0,56},{8,48},{16,8},{24,0},{32,24},{40,16},{48,40},{56,32},{64,12... | collective-permute-start | bytes 1572872 | tf_op jit(solution)/shard_map/ppermute | solution.py:41
  60.0 7.7 %collective-permute-done.4.refs_2_ = bf16[512,512]{1,0:T(8,128)(2,1)} collective-permute-done((bf16[512,512]{1,0:T(8,128)(2,1)}, bf16[512,512]{1,0:T(8,128)(2,1)}, u32[]{:S(2)}, u32[]{:S(2)}) %collective-permute-start.4) | collective-permute-done | bytes 524320 | tf_op jit(solution)/shard_map/ppermute | solution.py:41
  67.7 31.1 %shard_map.114 = (f32[2,4,512,128]{3,2,1,0:T(8,128)}, f32[2,4,512,128]{3,2,1,0:T(8,128)}) custom-call(s32[19]{0:T(128)} %stack.76.refs_0_, bf16[1024,512]{1,0:T(8,128)(2,1)} %refs_1_.3, bf16[512,512]{1,0:T(8,128)(2,1)} %collective-permute-done.4.refs_2_, bf16[1024,256]{1,0:T(8,128)(2,1)} %constant_dynamic-update-slice_fusion.refs_3_, ...), custom_call_target="tpu_custom_call" | custom-call | flops 34359738368 | bytes 16777216 | tf_op jit(solution)/shard_map/pallas_call | solution.py:208
  99.9 24.8 %shard_map.115 = (bf16[1024,512]{1,0:T(8,128)(2,1)}, bf16[512,512]{1,0:T(8,128)(2,1)}) custom-call(s32[19]{0:T(128)} %stack.76.refs_0_, bf16[1024,512]{1,0:T(8,128)(2,1)} %refs_1_.3, bf16[512,512]{1,0:T(8,128)(2,1)} %collective-permute-done.4.refs_2_, bf16[1536,256]{1,0:T(8,128)(2,1)} %copy-done, bf16[1536,256]{1,0:T(8,128)(2,1)} %copy-done.1, ...), custom_call_target="tpu_custom_call" | custom-call | flops 1 | bytes 1 | tf_op jit(solution)/shard_map/pallas_call | solution.py:208
  124.7 3.6 %collective-permute-start.11 = (bf16[512,512]{1,0:T(8,128)(2,1)}, bf16[512,512]{1,0:T(8,128)(2,1)S(1)}, u32[]{:S(2)}, u32[]{:S(2)}) collective-permute-start(bf16[512,512]{1,0:T(8,128)(2,1)} %get-tuple-element.30), channel_id=1, source_target_pairs={{0,120},{8,112},{16,104},{24,96},{32,88},{40,80},{48,72},{56,64},{... | collective-permute-start | bytes 1572872 | tf_op jit(solution)/shard_map/ppermute | solution.py:41
  128.2 2.3 %shard_map.116 = bf16[8,8,128]{2,1,0:T(8,128)(2,1)} custom-call(bf16[16,8,16,128]{3,2,1,0:T(8,128)(2,1)} %bitcast.27, bf16[8,8,128]{2,1,0:T(8,128)(2,1)} %bitcast.30, bf16[2,8,128]{2,1,0:T(8,128)(2,1)} %k_ref.3, bf16[2,8,128]{2,1,0:T(8,128)(2,1)} %v_ref.3), custom_call_target="tpu_custom_call" | custom-call | flops 1 | bytes 1 | tf_op jit(solution)/shard_map/pallas_call | solution.py:348
  131.9 10.7 %collective-permute-done.11 = bf16[512,512]{1,0:T(8,128)(2,1)S(1)} collective-permute-done((bf16[512,512]{1,0:T(8,128)(2,1)}, bf16[512,512]{1,0:T(8,128)(2,1)S(1)}, u32[]{:S(2)}, u32[]{:S(2)}) %collective-permute-start.11) | collective-permute-done | bytes 524320 | tf_op jit(solution)/shard_map/ppermute | solution.py:41
  (55 shorter events, 6.4 us)
Async XLA Ops:
  4.0 22.8 %collective-permute-start = (bf16[1024,256]{1,0:T(8,128)(2,1)}, bf16[1024,256]{1,0:T(8,128)(2,1)S(1)}, u32[]{:S(2)}, u32[]{:S(2)}) collective-permute-start(bf16[1024,256]{1,0:T(8,128)(2,1)} %constant_dynamic-update-slice_fusion.refs_3_), channel_id=1, source_target_pairs={{0,16},{8,24},{16,32},{24,40},{32,48},{40,56},{48,0},{56,8},{64,80... | collective-permute-start | bytes 1572872 | tf_op jit(solution)/shard_map/ppermute | solution.py:41
  6.1 20.7 %collective-permute-start.1 = (bf16[1024,256]{1,0:T(8,128)(2,1)}, bf16[1024,256]{1,0:T(8,128)(2,1)S(1)}, u32[]{:S(2)}, u32[]{:S(2)}) collective-permute-start(bf16[1024,256]{1,0:T(8,128)(2,1)} %constant_dynamic-update-slice_fusion.refs_3_), channel_id=1, source_target_pairs={{0,48},{8,56},{16,0},{24,8},{32,16},{40,24},{48,32},{56,40},{64,11... | collective-permute-start | bytes 1572872 | tf_op jit(solution)/shard_map/ppermute | solution.py:41
  7.6 19.3 %collective-permute-start.2 = (bf16[1024,256]{1,0:T(8,128)(2,1)}, bf16[1024,256]{1,0:T(8,128)(2,1)S(1)}, u32[]{:S(2)}, u32[]{:S(2)}) collective-permute-start(bf16[1024,256]{1,0:T(8,128)(2,1)} %constant_dynamic-update-slice_fusion.refs_3_), channel_id=1, source_target_pairs={{0,64},{8,72},{16,80},{24,88},{32,96},{40,104},{48,112},{56,120},{... | collective-permute-start | bytes 1572872 | tf_op jit(solution)/shard_map/ppermute | solution.py:41
  11.9 16.4 %copy-start.9 = (bf16[2,8,4,128]{3,2,0,1:T(4,128)(2,1)}, bf16[2,8,4,128]{3,2,0,1:T(4,128)(2,1)S(1)}, u32[]{:S(2)}) copy-start(bf16[2,8,4,128]{3,2,0,1:T(4,128)(2,1)S(1)} %copy.18) | copy-start | bytes 49156
  26.8 1.9 %copy-start.5 = (bf16[1024,256]{1,0:T(8,128)(2,1)}, bf16[1024,256]{1,0:T(8,128)(2,1)S(1)}, u32[]{:S(2)}) copy-start(bf16[1024,256]{1,0:T(8,128)(2,1)S(1)} %collective-permute-done.refs_5_) | copy-start | bytes 1572868
  26.8 1.9 %copy-start.6 = (bf16[1024,256]{1,0:T(8,128)(2,1)}, bf16[1024,256]{1,0:T(8,128)(2,1)S(1)}, u32[]{:S(2)}) copy-start(bf16[1024,256]{1,0:T(8,128)(2,1)S(1)} %collective-permute-done.1.refs_6_) | copy-start | bytes 1572868
  26.9 2.0 %copy-start.3 = (bf16[1024,256]{1,0:T(8,128)(2,1)}, bf16[1024,256]{1,0:T(8,128)(2,1)S(1)}, u32[]{:S(2)}) copy-start(bf16[1024,256]{1,0:T(8,128)(2,1)S(1)} %collective-permute-done.2.refs_7_) | copy-start | bytes 1572868
  28.3 6.1 %collective-permute-start.3 = (bf16[3072,256]{1,0:T(8,128)(2,1)}, bf16[3072,256]{1,0:T(8,128)(2,1)}, u32[]{:S(2)}, u32[]{:S(2)}) collective-permute-start(bf16[3072,256]{1,0:T(8,128)(2,1)} %pad_maximum_fusion), channel_id=1, source_target_pairs={{0,8},{8,0},{16,24},{24,16},{32,40},{40,32},{48,56},{56,48},{64,72... | collective-permute-start | bytes 4718600 | tf_op jit(solution)/shard_map/ppermute | solution.py:41
  28.3 31.8 %collective-permute-start.10 = (bf16[1024,256]{1,0:T(8,128)(2,1)}, bf16[1024,256]{1,0:T(8,128)(2,1)}, u32[]{:S(2)}, u32[]{:S(2)}) collective-permute-start(bf16[1024,256]{1,0:T(8,128)(2,1)} %constant_dynamic-update-slice_fusion.refs_3_), channel_id=1, source_target_pairs={{0,8},{8,0},{16,24},{24,16},{32,40},{40,32},{48,56},{56,48},{64,72... | collective-permute-start | bytes 1572872 | tf_op jit(solution)/shard_map/ppermute | solution.py:41
  28.8 3.7 %copy-start.11 = (s32[128]{0:T(128)S(1)}, s32[128]{0:T(128)}, u32[]{:S(2)}) copy-start(s32[128]{0:T(128)} %param.19) | copy-start | bytes 1540
  28.8 3.9 %copy-start.10 = (s32[128,16]{0,1:T(8,128)S(1)}, s32[128,16]{0,1:T(8,128)}, u32[]{:S(2)}) copy-start(s32[128,16]{0,1:T(8,128)} %param.18) | copy-start | bytes 24580
  29.8 25.1 %collective-permute-start.5 = (bf16[1536,256]{1,0:T(8,128)(2,1)}, bf16[1536,256]{1,0:T(8,128)(2,1)S(1)}, u32[]{:S(2)}, u32[]{:S(2)}) collective-permute-start(bf16[1536,256]{1,0:T(8,128)(2,1)} %get-tuple-element.35), channel_id=1, source_target_pairs={{0,16},{8,24},{16,32},{24,40},{32,48},{40,56},{48,0},{56,8},{64,80... | collective-permute-start | bytes 2359304 | tf_op jit(solution)/shard_map/ppermute | solution.py:41
  30.7 24.3 %collective-permute-start.6 = (bf16[1536,256]{1,0:T(8,128)(2,1)S(1)}, bf16[1536,256]{1,0:T(8,128)(2,1)S(1)}, u32[]{:S(2)}, u32[]{:S(2)}) collective-permute-start(bf16[1536,256]{1,0:T(8,128)(2,1)S(1)} %get-tuple-element.34), channel_id=1, source_target_pairs={{0,48},{8,56},{16,0},{24,8},{32,16},{40,24},{48,32},{56,40},{64,11... | collective-permute-start | bytes 2359304 | tf_op jit(solution)/shard_map/ppermute | solution.py:41
  34.3 11.5 %copy-start.2 = (bf16[1024,512]{1,0:T(8,128)(2,1)S(1)}, bf16[1024,512]{1,0:T(8,128)(2,1)}, u32[]{:S(2)}) copy-start(bf16[1024,512]{1,0:T(8,128)(2,1)} %refs_1_.3) | copy-start | bytes 3145732
  46.6 21.1 %collective-permute-start.4 = (bf16[512,512]{1,0:T(8,128)(2,1)}, bf16[512,512]{1,0:T(8,128)(2,1)}, u32[]{:S(2)}, u32[]{:S(2)}) collective-permute-start(bf16[512,512]{1,0:T(8,128)(2,1)} %slice.15), channel_id=1, source_target_pairs={{0,120},{8,112},{16,104},{24,96},{32,88},{40,80},{48,72},{56,64},{... | collective-permute-start | bytes 1572872 | tf_op jit(solution)/shard_map/ppermute | solution.py:41
  50.9 48.0 %all-to-all-start.1 = ((bf16[128,16,128]{2,1,0:T(8,128)(2,1)}), bf16[128,16,128]{2,1,0:T(8,128)(2,1)S(1)}, u32[]{:S(2)}, u32[]{:S(2)}) async-start(bf16[128,16,128]{2,1,0:T(8,128)(2,1)} %shard_map.113), calls=%async_computation.1 | async-start | bytes 1048576 | tf_op jit(solution)/shard_map/all_to_all | solution.py:400
  55.0 1.6 %copy-start = (bf16[1536,256]{1,0:T(8,128)(2,1)}, bf16[1536,256]{1,0:T(8,128)(2,1)S(1)}, u32[]{:S(2)}) copy-start(bf16[1536,256]{1,0:T(8,128)(2,1)S(1)} %collective-permute-done.5.refs_3_) | copy-start | bytes 2359300
  55.0 1.7 %copy-start.1 = (bf16[1536,256]{1,0:T(8,128)(2,1)}, bf16[1536,256]{1,0:T(8,128)(2,1)S(1)}, u32[]{:S(2)}) copy-start(bf16[1536,256]{1,0:T(8,128)(2,1)S(1)} %collective-permute-done.6.refs_4_) | copy-start | bytes 2359300
  56.7 42.2 %collective-permute-start.9 = (bf16[3072,256]{1,0:T(8,128)(2,1)}, bf16[3072,256]{1,0:T(8,128)(2,1)}, u32[]{:S(2)}, u32[]{:S(2)}) collective-permute-start(bf16[3072,256]{1,0:T(8,128)(2,1)} %pad_maximum_fusion.1), channel_id=1, source_target_pairs={{0,8},{8,0},{16,24},{24,16},{32,40},{40,32},{48,56},{56,48},{64,72... | collective-permute-start | bytes 4718600 | tf_op jit(solution)/shard_map/ppermute | solution.py:41
  56.8 42.0 %collective-permute-start.7 = (bf16[1024,256]{1,0:T(8,128)(2,1)S(1)}, bf16[1024,256]{1,0:T(8,128)(2,1)S(1)}, u32[]{:S(2)}, u32[]{:S(2)}) collective-permute-start(bf16[1024,256]{1,0:T(8,128)(2,1)S(1)} %slice.18), channel_id=1, source_target_pairs={{0,16},{8,24},{16,32},{24,40},{32,48},{40,56},{48,0},{56,8},{64,80... | collective-permute-start | bytes 1572872 | tf_op jit(solution)/shard_map/ppermute | solution.py:41
  58.4 40.4 %collective-permute-start.8 = (bf16[1024,256]{1,0:T(8,128)(2,1)S(1)}, bf16[1024,256]{1,0:T(8,128)(2,1)S(1)}, u32[]{:S(2)}, u32[]{:S(2)}) collective-permute-start(bf16[1024,256]{1,0:T(8,128)(2,1)S(1)} %slice.19), channel_id=1, source_target_pairs={{0,56},{8,48},{16,8},{24,0},{32,24},{40,16},{48,40},{56,32},{64,12... | collective-permute-start | bytes 1572872 | tf_op jit(solution)/shard_map/ppermute | solution.py:41
  98.8 25.9 %copy-start.4 = (bf16[128,16,128]{2,1,0:T(8,128)(2,1)}, bf16[128,16,128]{2,1,0:T(8,128)(2,1)S(1)}, u32[]{:S(2)}) copy-start(bf16[128,16,128]{2,1,0:T(8,128)(2,1)S(1)} %all-to-all-done.1) | copy-start | bytes 1572868
  98.9 1.0 copy-start.8
  124.7 17.9 %collective-permute-start.11 = (bf16[512,512]{1,0:T(8,128)(2,1)}, bf16[512,512]{1,0:T(8,128)(2,1)S(1)}, u32[]{:S(2)}, u32[]{:S(2)}) collective-permute-start(bf16[512,512]{1,0:T(8,128)(2,1)} %get-tuple-element.30), channel_id=1, source_target_pairs={{0,120},{8,112},{16,104},{24,96},{32,88},{40,80},{48,72},{56,64},{... | collective-permute-start | bytes 1572872 | tf_op jit(solution)/shard_map/ppermute | solution.py:41
  (1 other events, 0.8 us)
